TPU v7x, 32 devices: a whole 2x2x4 slice. The times are simulated.
32 devices in a mesh: grp: 2 (over y), ep: 4 (over z), dp: 4 (over x, core).
Axes of the slice: x: 2, y: 2, z: 4, core: 2. Of those that a mesh axis runs over, the one named last changes fastest.
Arguments:
- hidden_in: bfloat16 [2, 2048, 4096], P(None, ('grp', 'ep', 'dp')), parts along dimension 1, may hold values from -3 to 3
- norm_gain: bfloat16 [4096], replicated, may hold values from 0.099609375 to 1.8984375
- span_plan: int32 [2, 8, 8], P(None, ('grp', 'ep')), parts along dimension 1, may hold values from 0 to 7, each once within a row
- route_ids: int32 [2, 2048, 2], P(None, ('grp', 'ep', 'dp')), parts along dimension 1, may hold values from 0 to 3, all different within a row; in each aligned block of 256 rows (0 to 255, 256 to 511, ..., all dimensions but the last counted through in order) at most 192 rows name the same one
- route_gates: float32 [2, 2048, 2], P(None, ('grp', 'ep', 'dp')), parts along dimension 1, may hold values from 0.1 to 0.6
- w_gate: bfloat16 [4, 4096, 1536], P('ep', 'dp'), may hold values from -0.09375 to 0.09375
- w_up: bfloat16 [4, 4096, 1536], P('ep', 'dp'), may hold values from -0.09375 to 0.09375
- w_down: bfloat16 [4, 1536, 4096], P('ep', None, 'dp'), may hold values from -0.15625 to 0.15625
Outputs:
- mixed: bfloat16 [2, 2048, 4096], P(None, ('grp', 'ep', 'dp')), parts along dimension 1
There are 2 independent parts, one for each index of `grp`. A program takes and returns all parts, laid end to end along the dimension named above; an argument that names none is the same for every part. Nothing has to cross between parts.
Inputs may be any that keep to these rules, and one draw needn't show every extreme that they name: `route_ids`: in each micro-batch, the rows of one ep index (256 rows in a row, aligned) name any expert at most 192 times, a bound that some block reaches; a row names 2 different experts. `span_plan`: for each micro-batch and ep index, a permutation of the 8 spans of that ep index.
All inputs are finite; a program needn't handle non-finite values.
Results may differ from a plain program's by a relative error of at most 0.012.
Values may be sent and summed in bfloat16 or wider, within the bound.
A program may use at most 128 MiB of HBM per device.

v0:
```python
import jax
import jax.numpy as jnp
from jax import lax
from jax.sharding import PartitionSpec as P

SPANS = 2


def rms_norm(values, norm_gain):
    wide = values.astype(jnp.float32)
    factor = lax.rsqrt(jnp.mean(wide * wide, -1, keepdims=True) + 1e-06)
    return (wide * factor * norm_gain.astype(jnp.float32)).astype(jnp.bfloat16)


def permute_spans(values, order):
    pieces = values.reshape((order.shape[0], -1) + values.shape[1:])
    return jnp.take(pieces, order, axis=0).reshape(values.shape)


def send_both(values, norm_gain):
    normed = rms_norm(values, norm_gain)
    return (
        lax.all_to_all(values, "dp", split_axis=1, concat_axis=0, tiled=True),
        lax.all_to_all(normed, "dp", split_axis=1, concat_axis=0, tiled=True),
    )


def expert_block(received, w_gate, w_up, w_down):
    slot_count = received.shape[0]
    gate_shard = w_gate[0]
    up_local = w_up[0]
    down_local = w_down[0]
    dims = (((0,), (1,)), ((), ()))
    gate_part = lax.dot_general(gate_shard, received, dims, preferred_element_type=jnp.float32)
    up_part = lax.dot_general(up_local, received, dims, preferred_element_type=jnp.float32)
    summed = lax.psum_scatter(
        jnp.concatenate([gate_part, up_part], 1).astype(jnp.bfloat16),
        "dp",
        scatter_dimension=0,
        tiled=True,
    ).astype(jnp.float32)
    hidden = (jax.nn.silu(summed[:, :slot_count]) * summed[:, slot_count:]).astype(jnp.bfloat16)
    block_output = lax.dot_general(
        lax.all_gather(hidden, "dp", axis=0, tiled=True),
        down_local,
        (((0,), (0,)), ((), ())),
        preferred_element_type=jnp.float32,
    )
    return block_output.astype(jnp.bfloat16)


def layer_block(feat_values, feat_normed, group_ids, group_gates, w_gate, w_up, w_down, ep_count):
    group_rows, feat_width = feat_normed.shape
    route_count = group_ids.shape[1]
    expert_capacity = 3 * group_rows * route_count // (2 * ep_count)
    slot_count = ep_count * expert_capacity
    flat_ids = group_ids.reshape(-1)
    onehot = (flat_ids[:, None] == jnp.arange(ep_count, dtype=jnp.int32)[None, :]).astype(jnp.int32)
    position = jnp.sum((jnp.cumsum(onehot, 0) - 1) * onehot, 1)
    slot_of = flat_ids * expert_capacity + position
    token_of = jnp.arange(flat_ids.shape[0], dtype=jnp.int32) // route_count
    table = jnp.full((slot_count,), group_rows, jnp.int32).at[slot_of].set(token_of)
    padded = jnp.concatenate([feat_normed, jnp.zeros((1, feat_width), jnp.bfloat16)], 0)
    outgoing = padded[table].reshape(ep_count, expert_capacity, feat_width)
    received = lax.all_to_all(outgoing, "ep", split_axis=0, concat_axis=0, tiled=True).reshape(
        slot_count, feat_width
    )
    expert_out = expert_block(received, w_gate, w_up, w_down)
    returned = lax.all_to_all(
        expert_out.reshape(ep_count, expert_capacity, feat_width),
        "ep",
        split_axis=0,
        concat_axis=0,
        tiled=True,
    )
    picked = returned.reshape(slot_count, feat_width)[slot_of].reshape(
        group_rows, route_count, feat_width
    )
    moe_sum = jnp.sum(picked.astype(jnp.float32) * group_gates[:, :, None], 1)
    combined = (feat_values.astype(jnp.float32) + moe_sum).astype(jnp.bfloat16)
    return lax.all_to_all(combined, "dp", split_axis=0, concat_axis=1, tiled=True)


def local(hidden_in, norm_gain, span_plan, route_ids, route_gates, w_gate, w_up, w_down):
    dp_count = lax.axis_size("dp")
    ep_count = lax.axis_size("ep")
    dp_rank = lax.axis_index("dp")
    batch_groups, tok_rows, width = hidden_in.shape
    span_rows = tok_rows // SPANS
    all_ids, all_gates = (
        lax.all_gather(route_ids, "dp", axis=1, tiled=True),
        lax.all_gather(route_gates, "dp", axis=1, tiled=True),
    )
    plan_rows = span_plan[:, 0, :]
    features = []
    ids_now = []
    gates_now = []
    late_order = []
    pooled = lax.all_gather(hidden_in, "dp", axis=1, tiled=True)
    own_plan = lax.dynamic_slice_in_dim(plan_rows, dp_rank * SPANS, SPANS, 1)
    for batch_index in range(batch_groups):
        ids_now.append(permute_spans(all_ids[batch_index], plan_rows[batch_index]))
        gates_now.append(permute_spans(all_gates[batch_index], plan_rows[batch_index]))
        late_order.append(None)
        pieces = pooled[batch_index].reshape(dp_count * SPANS, span_rows, width)
        own_rows = jnp.take(pieces, own_plan[batch_index], axis=0).reshape(tok_rows, width)
        features.append(send_both(own_rows, norm_gain))
    outputs = []
    for batch_index in range(batch_groups):
        feat_values, feat_normed = features[batch_index]
        outputs.append(
            layer_block(
                feat_values,
                feat_normed,
                ids_now[batch_index],
                gates_now[batch_index],
                w_gate,
                w_up,
                w_down,
                ep_count,
            )
        )
    return jnp.stack(outputs, 0)


def solution(mesh):
    return jax.shard_map(
        local,
        mesh=mesh,
        in_specs=(
            P(None, ("grp", "ep", "dp"), None),
            P(),
            P(None, ("grp", "ep"), None),
            P(None, ("grp", "ep", "dp"), None),
            P(None, ("grp", "ep", "dp"), None),
            P("ep", "dp", None),
            P("ep", "dp", None),
            P("ep", None, "dp"),
        ),
        out_specs=P(None, ("grp", "ep", "dp"), None),
        check_vma=False,
    )
```

profile of v0, /device:TPU:0, one launch (start us, length us, event | category | flops | bytes accessed | tf_op | source)
XLA Modules:
  0.0 445.4 jit_solution(10762242702891535321)
XLA Ops:
  8.2 7.2 %all_gather.16 = s32[2,256,2]{2,0,1:T(2,128)S(1)} all-gather(s32[2,64,2]{2,0,1:T(2,128)S(1)} %copy.91), channel_id=1, replica_groups=mesh['grp'=2,'ep'=4,'dp'=4] {'dp'}, dimensions={1}, use_global_device_ids=true | all-gather | bytes 5120 | tf_op jit(solution)/shard_map/all_gather | solution.py:91
  20.3 25.8 %all-gather.4.cloned.1.call-done = bf16[2,256,4096]{2,1,0:T(8,128)(2,1)} async-done(((bf16[2,64,4096]{2,1,0:T(8,128)(2,1)}), bf16[2,256,4096]{2,1,0:T(8,128)(2,1)}) %all-gather.4.cloned.1.call-update) | async-done | bytes 4194320 | tf_op jit(solution)/shard_map/all_gather | solution.py:99
  46.1 4.7 %fusion.43 = (bf16[1,256,4096]{2,1,0:T(8,128)(2,1)}, bf16[1,256,4096]{2,1,0:T(8,128)(2,1)}) fusion(bf16[2,256,4096]{2,1,0:T(8,128)(2,1)} %all-gather.4.cloned.1.call-done), kind=kLoop, calls=%fused_computation.106 | loop fusion | bytes 8388608 | tf_op jit(solution)/shard_map/slice | solution.py:105
  53.8 3.0 gather_fusion.7
  67.5 4.1 all-to-all-start.1
  74.2 6.4 %all-to-all-done.1 = bf16[64,4,1024]{2,0,1:T(8,128)(2,1)} async-done(((bf16[64,4,1024]{2,0,1:T(8,128)(2,1)}), bf16[64,4,1024]{2,0,1:T(8,128)(2,1)}, u32[]{:S(2)}, u32[]{:S(2)}) %all-to-all-start.1) | async-done | bytes 524320 | tf_op jit(solution)/shard_map/all_to_all | solution.py:24
  82.5 5.7 %gather_fusion = bf16[768,1024]{1,0:T(8,128)(2,1)} fusion(bf16[257,1024]{1,0:T(8,128)(2,1)} %concatenate.14, s32[1024]{0:T(1024)S(1)} %pad_clamp_fusion.5), kind=kCustom, calls=%fused_computation.6 | custom fusion | bytes 3148800 | tf_op jit(solution)/shard_map/gather | solution.py:64
  88.1 41.6 %all_to_all.104 = bf16[4,192,1024]{2,1,0:T(8,128)(2,1)S(1)} all-to-all(bf16[4,192,1024]{2,1,0:T(8,128)(2,1)} %bitcast.129), channel_id=1, replica_groups=mesh['grp'=2,'ep'=4,'dp'=4] {'ep'}, dimensions={0} | all-to-all | bytes 3145728 | tf_op jit(solution)/shard_map/all_to_all | solution.py:65
  137.9 6.6 %copy.127 = bf16[1536,1536]{1,0:T(8,128)(2,1)} copy(bf16[1536,1536]{0,1:T(8,128)(2,1)} %pad_maximum_fusion) | data formatting | bytes 9437184
  149.0 4.2 all-to-all-start.6
  156.0 6.2 %all-to-all-done.6 = bf16[64,4,1024]{2,0,1:T(8,128)(2,1)} async-done(((bf16[64,4,1024]{2,0,1:T(8,128)(2,1)}), bf16[64,4,1024]{2,0,1:T(8,128)(2,1)}, u32[]{:S(2)}, u32[]{:S(2)}) %all-to-all-start.6) | async-done | bytes 524320 | tf_op jit(solution)/shard_map/all_to_all | solution.py:24
  164.1 5.7 %gather_fusion.2 = bf16[768,1024]{1,0:T(8,128)(2,1)} fusion(bf16[257,1024]{1,0:T(8,128)(2,1)} %concatenate.16, s32[1024]{0:T(1024)S(1)} %pad_clamp_fusion.1), kind=kCustom, calls=%fused_computation.8 | custom fusion | bytes 3148800 | tf_op jit(solution)/shard_map/gather | solution.py:64
  169.8 40.6 %all_to_all.105 = bf16[4,192,1024]{2,1,0:T(8,128)(2,1)S(1)} all-to-all(bf16[4,192,1024]{2,1,0:T(8,128)(2,1)} %bitcast.130), channel_id=1, replica_groups=mesh['grp'=2,'ep'=4,'dp'=4] {'ep'}, dimensions={0} | all-to-all | bytes 3145728 | tf_op jit(solution)/shard_map/all_to_all | solution.py:65
  218.6 6.7 %copy.129 = bf16[1536,1536]{1,0:T(8,128)(2,1)} copy(bf16[1536,1536]{0,1:T(8,128)(2,1)} %pad_maximum_fusion.1) | data formatting | bytes 9437184
  230.7 40.8 %reduce-scatter.9.cloned.1.call-done = bf16[384,1536]{1,0:T(8,128)(2,1)} async-done(((bf16[1536,1536]{1,0:T(8,128)(2,1)}), bf16[384,1536]{1,0:T(8,128)(2,1)}) %reduce-scatter.9.cloned.1.call-update) | async-done | bytes 1179664
  277.4 3.5 all-to-all-start
  280.9 21.7 %all-gather.6.cloned.1.call-done = bf16[1536,768]{0,1:T(8,128)(2,1)} async-done(((bf16[384,768]{0,1:T(8,128)(2,1)}), bf16[1536,768]{0,1:T(8,128)(2,1)}) %all-gather.6.cloned.1.call-update) | async-done | bytes 2359312 | tf_op jit(solution)/shard_map/all_gather | solution.py:44
  302.6 6.3 %fusion.20 = bf16[768,1024]{1,0:T(8,128)(2,1)} fusion(bf16[1536,768]{0,1:T(8,128)(2,1)} %all-gather.6.cloned.1.call-done, bf16[1,1536,1024]{2,1,0:T(8,128)(2,1)} %param.21), kind=kOutput, calls=%fused_computation.32 | convolution fusion | flops 2416705536 | bytes 7077888 | tf_op jit(solution)/shard_map/dot_general | solution.py:43
  308.9 4.6 %all-to-all-start.3 = ((bf16[4,192,1024]{2,1,0:T(8,128)(2,1)}), bf16[4,192,1024]{2,1,0:T(8,128)(2,1)S(1)}, u32[]{:S(2)}, u32[]{:S(2)}) async-start(bf16[4,192,1024]{2,1,0:T(8,128)(2,1)} %bitcast.136), calls=%async_computation.3 | async-start | bytes 3145728 | tf_op jit(solution)/shard_map/all_to_all | solution.py:69
  313.5 14.5 %all-gather.8.cloned.1.call-done = bf16[1536,768]{0,1:T(8,128)(2,1)} async-done(((bf16[384,768]{0,1:T(8,128)(2,1)}), bf16[1536,768]{0,1:T(8,128)(2,1)}) %all-gather.8.cloned.1.call-update) | async-done | bytes 2359312 | tf_op jit(solution)/shard_map/all_gather | solution.py:44
  328.1 6.4 %fusion.23 = bf16[768,1024]{1,0:T(8,128)(2,1)} fusion(bf16[1536,768]{0,1:T(8,128)(2,1)} %all-gather.8.cloned.1.call-done, bf16[1,1536,1024]{2,1,0:T(8,128)(2,1)} %param.21), kind=kOutput, calls=%fused_computation.33 | convolution fusion | flops 2416705536 | bytes 7077888 | tf_op jit(solution)/shard_map/dot_general | solution.py:43
  334.4 16.5 %all-to-all-done.3 = bf16[4,192,1024]{2,1,0:T(8,128)(2,1)S(1)} async-done(((bf16[4,192,1024]{2,1,0:T(8,128)(2,1)}), bf16[4,192,1024]{2,1,0:T(8,128)(2,1)S(1)}, u32[]{:S(2)}, u32[]{:S(2)}) %all-to-all-start.3) | async-done | bytes 1572896 | tf_op jit(solution)/shard_map/all_to_all | solution.py:69
  350.9 3.6 all-to-all-start.8
  354.6 6.0 %all_gather.18 = f32[2,256,2]{2,0,1:T(2,128)S(1)} all-gather(f32[2,64,2]{2,0,1:T(2,128)S(1)} %copy.98), channel_id=1, replica_groups=mesh['grp'=2,'ep'=4,'dp'=4] {'dp'}, dimensions={1}, use_global_device_ids=true | all-gather | bytes 5120 | tf_op jit(solution)/shard_map/all_gather | solution.py:92
  367.3 3.4 reshape.244
  370.7 20.2 %all-to-all-done.8 = bf16[4,192,1024]{2,1,0:T(8,128)(2,1)S(1)} async-done(((bf16[4,192,1024]{2,1,0:T(8,128)(2,1)}), bf16[4,192,1024]{2,1,0:T(8,128)(2,1)S(1)}, u32[]{:S(2)}, u32[]{:S(2)}) %all-to-all-start.8) | async-done | bytes 1572896 | tf_op jit(solution)/shard_map/all_to_all | solution.py:69
  390.9 4.1 all-to-all-start.5
  395.1 5.3 %multiply_reduce_fusion.1 = f32[256,1024]{1,0:T(8,128)} fusion(f32[256,2,1024]{2,1,0:T(2,128)} %reshape.244, f32[256,2]{1,0:T(8,128)S(1)} %bitcast.142), kind=kLoop, calls=%fused_computation.31 | loop fusion | flops 786432 | bytes 3147776 | tf_op jit(solution)/shard_map/reduce_sum | solution.py:79
  406.0 4.1 all-to-all-start.4
  414.8 4.3 all-to-all-done.4
  419.1 4.1 all-to-all-start.9
  427.8 4.3 all-to-all-done.9
  (125 shorter events, 89.7 us)
Async XLA Ops:
  6.5 126.1 %copy-start = (bf16[1,1024,1536]{2,1,0:T(8,128)(2,1)S(1)}, bf16[1,1024,1536]{2,1,0:T(8,128)(2,1)}, u32[]{:S(2)}) copy-start(bf16[1,1024,1536]{2,1,0:T(8,128)(2,1)} %param.19) | copy-start | bytes 9437188
  6.5 13.6 %copy-start.5 = (s32[2,1,8]{2,1,0:T(1,128)S(1)}, s32[2,1,8]{2,1,0:T(1,128)}, u32[]{:S(2)}) copy-start(s32[2,1,8]{2,1,0:T(1,128)} %param.16) | copy-start | bytes 196
  6.5 11.6 %copy-start.4 = (bf16[4096]{0:T(1024)(128)(2,1)S(1)}, bf16[4096]{0:T(1024)(128)(2,1)}, u32[]{:S(2)}) copy-start(bf16[4096]{0:T(1024)(128)(2,1)} %param.15) | copy-start | bytes 24580
  6.5 39.6 %all-gather.4.cloned.1.call-start = ((), (), s32[]{:S(2)}) async-start(), calls=%async_computation.12 | async-start | bytes 5242880 | tf_op jit(solution)/shard_map/all_gather | solution.py:99
  67.5 13.1 %all-to-all-start.1 = ((bf16[64,4,1024]{2,0,1:T(8,128)(2,1)}), bf16[64,4,1024]{2,0,1:T(8,128)(2,1)}, u32[]{:S(2)}, u32[]{:S(2)}) async-start(bf16[64,4,1024]{2,0,1:T(8,128)(2,1)} %copy.90), calls=%async_computation.1 | async-start | bytes 1048576 | tf_op jit(solution)/shard_map/all_to_all | solution.py:24
  71.7 153.7 %reduce-scatter.7.cloned.1.call-start = ((), (), s32[]{:S(2)}) async-start(), calls=%async_computation.15 | async-start | bytes 5898240
  88.1 41.6 %copy-start.7 = (bf16[1,1024,1536]{2,1,0:T(8,128)(2,1)S(1)}, bf16[1,1024,1536]{2,1,0:T(8,128)(2,1)}, u32[]{:S(2)}) copy-start(bf16[1,1024,1536]{2,1,0:T(8,128)(2,1)} %param.20) | copy-start | bytes 9437188
  149.0 13.1 %all-to-all-start.6 = ((bf16[64,4,1024]{2,0,1:T(8,128)(2,1)}), bf16[64,4,1024]{2,0,1:T(8,128)(2,1)}, u32[]{:S(2)}, u32[]{:S(2)}) async-start(bf16[64,4,1024]{2,0,1:T(8,128)(2,1)} %copy.105), calls=%async_computation.6 | async-start | bytes 1048576 | tf_op jit(solution)/shard_map/all_to_all | solution.py:24
  153.2 118.2 %reduce-scatter.9.cloned.1.call-start = ((), (), s32[]{:S(2)}) async-start(), calls=%async_computation.16 | async-start | bytes 5898240
  210.4 2.8 copy-start.8
  225.4 77.2 %all-gather.6.cloned.1.call-start = ((), (), s32[]{:S(2)}) async-start(), calls=%async_computation.13 | async-start | bytes 2949120 | tf_op jit(solution)/shard_map/all_gather | solution.py:44
  230.6 97.4 %all-gather.8.cloned.1.call-start = ((), (), s32[]{:S(2)}) async-start(), calls=%async_computation.14 | async-start | bytes 2949120 | tf_op jit(solution)/shard_map/all_gather | solution.py:44
  275.2 1.2 copy-start.2
  277.4 31.5 %all-to-all-start = ((bf16[64,4,1024]{2,0,1:T(8,128)(2,1)}), bf16[64,4,1024]{2,0,1:T(8,128)(2,1)S(1)}, u32[]{:S(2)}, u32[]{:S(2)}) async-start(bf16[64,4,1024]{2,0,1:T(8,128)(2,1)} %copy.89), calls=%async_computation | async-start | bytes 1048576 | tf_op jit(solution)/shard_map/all_to_all | solution.py:23
  308.9 25.5 %copy-start.3 = (bf16[64,4,1024]{2,0,1:T(8,128)(2,1)}, bf16[64,4,1024]{2,0,1:T(8,128)(2,1)S(1)}, u32[]{:S(2)}) copy-start(bf16[64,4,1024]{2,0,1:T(8,128)(2,1)S(1)} %all-to-all-done) | copy-start | bytes 1572868
  308.9 42.0 %all-to-all-start.3 = ((bf16[4,192,1024]{2,1,0:T(8,128)(2,1)}), bf16[4,192,1024]{2,1,0:T(8,128)(2,1)S(1)}, u32[]{:S(2)}, u32[]{:S(2)}) async-start(bf16[4,192,1024]{2,1,0:T(8,128)(2,1)} %bitcast.136), calls=%async_computation.3 | async-start | bytes 3145728 | tf_op jit(solution)/shard_map/all_to_all | solution.py:69
  334.4 20.0 %copy-start.6 = (f32[2,64,2]{1,2,0:T(2,128)S(1)}, f32[2,64,2]{1,2,0:T(2,128)}, u32[]{:S(2)}) copy-start(f32[2,64,2]{1,2,0:T(2,128)} %param.18) | copy-start | bytes 3076
  350.9 40.1 %all-to-all-start.8 = ((bf16[4,192,1024]{2,1,0:T(8,128)(2,1)}), bf16[4,192,1024]{2,1,0:T(8,128)(2,1)S(1)}, u32[]{:S(2)}, u32[]{:S(2)}) async-start(bf16[4,192,1024]{2,1,0:T(8,128)(2,1)} %bitcast.135), calls=%async_computation.8 | async-start | bytes 3145728 | tf_op jit(solution)/shard_map/all_to_all | solution.py:69
  390.9 15.1 %all-to-all-start.5 = ((bf16[64,4,1024]{2,0,1:T(8,128)(2,1)}), bf16[64,4,1024]{2,0,1:T(8,128)(2,1)}, u32[]{:S(2)}, u32[]{:S(2)}) async-start(bf16[64,4,1024]{2,0,1:T(8,128)(2,1)} %copy.104), calls=%async_computation.5 | async-start | bytes 1048576 | tf_op jit(solution)/shard_map/all_to_all | solution.py:23
  406.0 13.0 %all-to-all-start.4 = ((bf16[4,64,1024]{2,1,0:T(8,128)(2,1)}), bf16[4,64,1024]{2,1,0:T(8,128)(2,1)}, u32[]{:S(2)}, u32[]{:S(2)}) async-start(bf16[4,64,1024]{2,1,0:T(8,128)(2,1)} %fusion.29), calls=%async_computation.4 | async-start | bytes 1048576 | tf_op jit(solution)/shard_map/all_to_all | solution.py:81
  419.1 13.0 %all-to-all-start.9 = ((bf16[4,64,1024]{2,1,0:T(8,128)(2,1)}), bf16[4,64,1024]{2,1,0:T(8,128)(2,1)}, u32[]{:S(2)}, u32[]{:S(2)}) async-start(bf16[4,64,1024]{2,1,0:T(8,128)(2,1)} %fusion.28), calls=%async_computation.9 | async-start | bytes 1048576 | tf_op jit(solution)/shard_map/all_to_all | solution.py:81
  425.5 13.4 %copy-start.1 = (bf16[1,1024,1536]{2,1,0:T(8,128)(2,1)S(1)}, bf16[1,1024,1536]{2,1,0:T(8,128)(2,1)}, u32[]{:S(2)}) copy-start(bf16[1,1024,1536]{2,1,0:T(8,128)(2,1)} %param.19) | copy-start | bytes 9437188
Sparse Core Ops, SparseCore 0:
  8.9 37.1 all-gather.3
  144.7 46.1 reduce-scatter.6
  225.5 45.9 reduce-scatter.8
  272.9 29.6 all-gather.5
  304.0 24.0 all-gather.7
where the time goes:
time: 447 us; the launch traced here: 445 us
  waiting for transfers between devices  161 us (36%)
  blocking collectives  95.5 us (21%)
  local copies, waits for them, and re-layouts  84.4 us (19%)
  other arithmetic  34 us (8%)
  starting transfers between devices  32.6 us (7%)
  matrix products  24 us (5%)
  between operations  13.5 us (3%)
    all_to_all x2, blocking collectives, layer_block(): lax.all_to_all(outgoing, 'ep', split_axis=0, concat_axis=0, tiled=True)  82.3 us
    unnamed x7, waiting for transfers between devices  41.6 us
    all_to_all x2, waiting for transfers between devices, layer_block(): lax.all_to_all(expert_out.reshape(ep_count, expert_capacity, feat_width),...  36.7 us
    all_gather x2, waiting for transfers between devices, expert_block(): lax.all_gather(hidden, 'dp', axis=0, tiled=True)  36.2 us
    all_gather x1, waiting for transfers between devices, local(): pooled = lax.all_gather(hidden_in, 'dp', axis=1, tiled=True)  25.8 us
    unnamed x24, local copies, waits for them, and re-layouts  19.1 us
    dot_general x2, matrix products, expert_block(): lax.dot_general(lax.all_gather(hidden, 'dp', axis=0, tiled=True), down_lo...  12.7 us
    all_to_all x2, waiting for transfers between devices, send_both(): lax.all_to_all(normed, 'dp', split_axis=1, concat_axis=0, tiled=True)  12.5 us
  transfers between devices with their start and end apart: 13, of which 10 were waited for; matrix products, arithmetic and copies ran while one was open for 21% of the time, Pallas kernels for 0%

commit v1 on v0

v1 whole, which is shorter than its diff:
```python
import jax
import jax.numpy as jnp
from jax import lax
from jax.sharding import PartitionSpec as P

SPANS = 2


def dot32(left, right):
    return jnp.dot(left, right, preferred_element_type=jnp.float32)


def slots_of(ids, ep_count):
    experts = jnp.arange(ep_count, dtype=jnp.float32)
    named = sum((ids[:, r : r + 1] == experts[None, :]).astype(jnp.float32) for r in range(ids.shape[1]))
    rows = ids.shape[0]
    earlier = jnp.arange(rows)[:, None] > jnp.arange(rows)[None, :]
    place = dot32(earlier.astype(jnp.bfloat16), named.astype(jnp.bfloat16))
    return named, place


def local(hidden_in, norm_gain, span_plan, route_ids, route_gates, w_gate, w_up, w_down):
    dp_count = lax.axis_size("dp")
    ep_count = lax.axis_size("ep")
    dp_rank = lax.axis_index("dp")
    batches, tok_rows, width = hidden_in.shape
    routes = route_ids.shape[2]
    span_rows = tok_rows // SPANS
    group_rows = dp_count * tok_rows
    feat = width // dp_count
    hidden_units = w_gate.shape[2]
    capacity = 3 * group_rows * routes // (2 * ep_count)
    slot_count = ep_count * capacity

    split = hidden_in.reshape(batches, tok_rows, dp_count, feat).transpose(2, 0, 1, 3)
    values = lax.all_to_all(split, "dp", split_axis=0, concat_axis=0, tiled=True)
    wide = hidden_in.astype(jnp.float32)
    factor = lax.rsqrt(jnp.mean(wide * wide, -1, keepdims=True) + 1e-06)
    facts = jnp.concatenate([factor, route_ids.astype(jnp.float32), route_gates], -1)
    facts = lax.all_gather(facts, "dp", axis=1, tiled=True)
    gain = lax.dynamic_slice_in_dim(norm_gain, dp_rank * feat, feat, 0).astype(jnp.float32)
    w_both = jnp.concatenate([w_gate[0], w_up[0]], 1)
    w_out = w_down[0]

    experts = jnp.arange(ep_count, dtype=jnp.float32)
    slot_place = jnp.arange(capacity, dtype=jnp.float32)
    rows_in = []
    mixers = []
    received = []
    for m in range(batches):
        rows = values[:, m].reshape(group_rows, feat)
        ids = facts[m, :, 1 : 1 + routes]
        gates = facts[m, :, 1 + routes :]
        normed = (rows.astype(jnp.float32) * facts[m, :, :1] * gain).astype(jnp.bfloat16)
        named, place = slots_of(ids, ep_count)
        where = jnp.where(named > 0, place, -1.0)
        pick = (where.T[:, None, :] == slot_place[None, :, None]).astype(jnp.bfloat16)
        outgoing = dot32(pick.reshape(slot_count, group_rows), normed).astype(jnp.bfloat16)
        received.append(
            lax.all_to_all(
                outgoing.reshape(ep_count, capacity, feat), "ep", split_axis=0, concat_axis=0, tiled=True
            ).reshape(slot_count, feat)
        )
        weight = sum(
            jnp.where(ids[:, r : r + 1] == experts[None, :], gates[:, r : r + 1], 0.0) for r in range(routes)
        )
        plan = span_plan[m, 0]
        table = jnp.concatenate([where, weight], 1).reshape(-1, span_rows, 2 * ep_count)
        table = jnp.take(table, plan, axis=0).reshape(group_rows, 2 * ep_count)
        spread = jnp.where(
            table[:, :ep_count, None] == slot_place[None, None, :], table[:, ep_count:, None], 0.0
        ).reshape(group_rows, slot_count)
        high = spread.astype(jnp.bfloat16)
        low = (spread - high.astype(jnp.float32)).astype(jnp.bfloat16)
        source = (plan[:, None] * span_rows + jnp.arange(span_rows)[None, :]).reshape(-1)
        order = (source[:, None] == jnp.arange(group_rows)[None, :]).astype(jnp.bfloat16)
        mixers.append((high, low, order))
        rows_in.append(rows)

    summed = []
    for m in range(batches):
        parts = dot32(received[m], w_both).astype(jnp.bfloat16)
        summed.append(lax.psum_scatter(parts, "dp", scatter_dimension=0, tiled=True).astype(jnp.float32))
    returned = []
    for m in range(batches):
        hidden = (jax.nn.silu(summed[m][:, :hidden_units]) * summed[m][:, hidden_units:]).astype(jnp.bfloat16)
        hidden = lax.all_gather(hidden, "dp", axis=0, tiled=True)
        expert_out = dot32(hidden, w_out).astype(jnp.bfloat16)
        returned.append(
            lax.all_to_all(
                expert_out.reshape(ep_count, capacity, feat), "ep", split_axis=0, concat_axis=0, tiled=True
            ).reshape(slot_count, feat)
        )
    outputs = []
    for m in range(batches):
        high, low, order = mixers[m]
        total = dot32(high, returned[m]) + dot32(low, returned[m]) + dot32(order, rows_in[m])
        combined = total.astype(jnp.bfloat16).reshape(dp_count, tok_rows, feat)
        outputs.append(lax.all_to_all(combined, "dp", split_axis=0, concat_axis=0, tiled=True))
    return jnp.stack(outputs, 0).transpose(0, 2, 1, 3).reshape(batches, tok_rows, width)


def solution(mesh):
    return jax.shard_map(
        local,
        mesh=mesh,
        in_specs=(
            P(None, ("grp", "ep", "dp"), None),
            P(),
            P(None, ("grp", "ep"), None),
            P(None, ("grp", "ep", "dp"), None),
            P(None, ("grp", "ep", "dp"), None),
            P("ep", "dp", None),
            P("ep", "dp", None),
            P("ep", None, "dp"),
        ),
        out_specs=P(None, ("grp", "ep", "dp"), None),
        check_vma=False,
    )
```

time: 447 us -> 341 us (0.76)
  local copies, waits for them, and re-layouts: 84.4 us -> 15.6 us
  waiting for transfers between devices: 161 us -> 129 us
  other arithmetic: 34 us -> 12.7 us
  matrix products: 24 us -> 41.3 us
  starting transfers between devices: 32.6 us -> 17.8 us
  blocking collectives: 95.5 us -> 109 us
    reduce_scatter x0 -> x2, waiting for transfers between devices: none -> 43.5 us  [local(): lax.psum_scatter(parts, 'dp', scatter_dimension=0, tiled=True)]
    unnamed x7 -> x4, waiting for transfers between devices: 41.6 us -> 0.07 us
    all_gather x3 -> x2, waiting for transfers between devices: 62 us -> 37.5 us  [local(): hidden = lax.all_gather(hidden, 'dp', axis=0, tiled=True)]
    gather x10 -> x2, local copies, waits for them, and re-layouts: 24.4 us -> 1.11 us  [local(): table = jnp.take(table, plan, axis=0).reshape(group_rows, 2 * ep_count)]
    unnamed x24 -> x17, local copies, waits for them, and re-layouts: 19.1 us -> 0.15 us
    dot_general x6 -> x14, matrix products: 24 us -> 41.3 us  [dot32(): return jnp.dot(left, right, preferred_element_type=jnp.float32)]
    all_to_all x8 -> x4, starting transfers between devices: 32.4 us -> 17.5 us  [the longest x2 9.08 us: local(): lax.all_to_all(expert_out.reshape(ep_count, capacity, feat), 'ep', split_...]
    all_to_all x2 -> x3, blocking collectives: 82.3 us -> 94.4 us  [the longest x2 82.1 us: local(): lax.all_to_all(outgoing.reshape(ep_count, capacity, feat), 'ep', split_ax...]
  transfers between devices with their start and end apart: 13 -> 8, of which waited for: 10 -> 6; matrix products, arithmetic and copies ran while one was open for 21% -> 15% of each run, Pallas kernels for 0% -> 0%
where the time goes in v1:
time: 341 us; the launch traced here: 340 us
  waiting for transfers between devices  129 us (38%)
  blocking collectives  109 us (32%)
  matrix products  41.3 us (12%)
  starting transfers between devices  17.8 us (5%)
  local copies, waits for them, and re-layouts  15.6 us (5%)
  between operations  13.4 us (4%)
  other arithmetic  12.7 us (4%)
    all_to_all x2, blocking collectives, local(): lax.all_to_all(outgoing.reshape(ep_count, capacity, feat), 'ep', split_ax...  82.1 us
    all_to_all x2, waiting for transfers between devices, local(): lax.all_to_all(expert_out.reshape(ep_count, capacity, feat), 'ep', split_...  44.8 us
    reduce_scatter x2, waiting for transfers between devices, local(): lax.psum_scatter(parts, 'dp', scatter_dimension=0, tiled=True)  43.5 us
    dot_general x14, matrix products, dot32(): return jnp.dot(left, right, preferred_element_type=jnp.float32)  41.3 us
    all_gather x2, waiting for transfers between devices, local(): hidden = lax.all_gather(hidden, 'dp', axis=0, tiled=True)  37.5 us
    all_gather x1, blocking collectives, local(): facts = lax.all_gather(facts, 'dp', axis=1, tiled=True)  15.1 us
    all_to_all x1, blocking collectives, local(): lax.all_to_all(combined, 'dp', split_axis=0, concat_axis=0, tiled=True)  12.3 us
    all_to_all x2, starting transfers between devices, local(): lax.all_to_all(expert_out.reshape(ep_count, capacity, feat), 'ep', split_...  9.08 us
  transfers between devices with their start and end apart: 8, of which 6 were waited for; matrix products, arithmetic and copies ran while one was open for 15% of the time, Pallas kernels for 0%

profile of v1, /device:TPU:0, one launch (start us, length us, event | category | flops | bytes accessed | tf_op | source)
XLA Modules:
  0.0 339.8 jit_solution(17922294974935186271)
XLA Ops:
  6.5 2.8 reshape.246
  9.3 2.5 copy.67
  11.9 4.3 %all-to-all-start = ((bf16[4,2,64,1024]{3,2,1,0:T(8,128)(2,1)}), bf16[4,2,64,1024]{3,2,1,0:T(8,128)(2,1)}, u32[]{:S(2)}, u32[]{:S(2)}) async-start(bf16[4,2,64,1024]{3,2,1,0:T(8,128)(2,1)} %copy.67), calls=%async_computation | async-start | bytes 2097152 | tf_op jit(solution)/shard_map/all_to_all | solution.py:36
  16.2 1.5 multiply_reduce_fusion
  18.3 15.1 %all_gather.9 = f32[2,256,5]{2,0,1:T(2,128)S(1)} all-gather(f32[2,64,5]{2,0,1:T(2,128)S(1)} %pad_maximum_fusion.3), channel_id=1, replica_groups=mesh['grp'=2,'ep'=4,'dp'=4] {'dp'}, dimensions={1}, use_global_device_ids=true | all-gather | bytes 12800 | tf_op jit(solution)/shard_map/all_gather | solution.py:40
  33.4 1.8 fusion.55
  36.4 1.9 slice_reduce_fusion.2
  40.6 2.4 multiply_convert_fusion.1
  43.0 1.7 convolution_convert_fusion.2
  44.7 43.0 %all_to_all.35 = bf16[4,192,1024]{2,1,0:T(8,128)(2,1)S(1)} all-to-all(bf16[4,192,1024]{2,1,0:T(8,128)(2,1)S(1)} %bitcast.90), channel_id=1, replica_groups=mesh['grp'=2,'ep'=4,'dp'=4] {'ep'}, dimensions={0} | all-to-all | bytes 3145728 | tf_op jit(solution)/shard_map/all_to_all | solution.py:60
  87.6 7.0 %convolution_convert_fusion = bf16[768,3072]{1,0:T(8,128)(2,1)} fusion(bf16[768,1024]{1,0:T(8,128)(2,1)S(1)} %bitcast.102, bf16[1024,1536]{1,0:T(8,128)(2,1)S(1)} %bitcast.110, bf16[1024,1536]{1,0:T(8,128)(2,1)S(1)} %bitcast.113), kind=kOutput, calls=%fused_computation.3 | convolution fusion | flops 4846780416 | bytes 12582912 | tf_op jit(solution)/shard_map/dot_general | solution.py:10
  95.4 1.8 convolution_convert_fusion.3
  97.1 39.1 %all_to_all.36 = bf16[4,192,1024]{2,1,0:T(8,128)(2,1)S(1)} all-to-all(bf16[4,192,1024]{2,1,0:T(8,128)(2,1)S(1)} %bitcast.91), channel_id=1, replica_groups=mesh['grp'=2,'ep'=4,'dp'=4] {'ep'}, dimensions={0} | all-to-all | bytes 3145728 | tf_op jit(solution)/shard_map/all_to_all | solution.py:60
  136.2 8.6 %convolution_convert_fusion.1 = bf16[768,3072]{1,0:T(8,128)(2,1)} fusion(bf16[768,1024]{1,0:T(8,128)(2,1)S(1)} %bitcast.103, bf16[1024,1536]{1,0:T(8,128)(2,1)S(1)} %bitcast.111, bf16[1024,1536]{1,0:T(8,128)(2,1)} %bitcast.112), kind=kOutput, calls=%fused_computation.4 | convolution fusion | flops 4846780416 | bytes 12582912 | tf_op jit(solution)/shard_map/dot_general | solution.py:10
  144.9 1.5 convert_element_type.158
  147.9 43.5 %reduce-scatter.3.cloned.1.call-done = bf16[192,3072]{1,0:T(8,128)(2,1)} async-done(((bf16[768,3072]{1,0:T(8,128)(2,1)}), bf16[192,3072]{1,0:T(8,128)(2,1)}) %reduce-scatter.3.cloned.1.call-update) | async-done | bytes 1179664 | tf_op jit(solution)/shard_map/reduce_scatter | solution.py:83
  194.1 23.0 %all-gather.5.cloned.1.call-done = bf16[768,1536]{1,0:T(8,128)(2,1)} async-done(((bf16[192,1536]{1,0:T(8,128)(2,1)}), bf16[768,1536]{1,0:T(8,128)(2,1)}) %all-gather.5.cloned.1.call-update) | async-done | bytes 2359312 | tf_op jit(solution)/shard_map/all_gather | solution.py:87
  217.1 5.4 %fusion.7 = bf16[768,1024]{1,0:T(8,128)(2,1)} fusion(bf16[768,1536]{1,0:T(8,128)(2,1)} %all-gather.5.cloned.1.call-done, bf16[1,1536,1024]{2,1,0:T(8,128)(2,1)S(1)} %copy-done), kind=kOutput, calls=%fused_computation.11 | convolution fusion | flops 2416705536 | bytes 7077888 | tf_op jit(solution)/shard_map/dot_general | solution.py:10
  222.5 4.7 %all-to-all-start.5 = ((bf16[4,192,1024]{2,1,0:T(8,128)(2,1)}), bf16[4,192,1024]{2,1,0:T(8,128)(2,1)}, u32[]{:S(2)}, u32[]{:S(2)}) async-start(bf16[4,192,1024]{2,1,0:T(8,128)(2,1)} %bitcast.101), calls=%async_computation.7 | async-start | bytes 3145728 | tf_op jit(solution)/shard_map/all_to_all | solution.py:90
  228.0 14.6 %all-gather.3.cloned.1.call-done = bf16[768,1536]{1,0:T(8,128)(2,1)} async-done(((bf16[192,1536]{1,0:T(8,128)(2,1)}), bf16[768,1536]{1,0:T(8,128)(2,1)}) %all-gather.3.cloned.1.call-update) | async-done | bytes 2359312 | tf_op jit(solution)/shard_map/all_gather | solution.py:87
  242.6 5.4 %fusion.4 = bf16[768,1024]{1,0:T(8,128)(2,1)} fusion(bf16[768,1536]{1,0:T(8,128)(2,1)} %all-gather.3.cloned.1.call-done, bf16[1,1536,1024]{2,1,0:T(8,128)(2,1)S(1)} %copy-done), kind=kOutput, calls=%fused_computation.10 | convolution fusion | flops 2416705536 | bytes 7077888 | tf_op jit(solution)/shard_map/dot_general | solution.py:10
  248.0 16.7 %all-to-all-done.5 = bf16[4,192,1024]{2,1,0:T(8,128)(2,1)} async-done(((bf16[4,192,1024]{2,1,0:T(8,128)(2,1)}), bf16[4,192,1024]{2,1,0:T(8,128)(2,1)}, u32[]{:S(2)}, u32[]{:S(2)}) %all-to-all-start.5) | async-done | bytes 1572896 | tf_op jit(solution)/shard_map/all_to_all | solution.py:90
  264.7 4.4 %all-to-all-start.2 = ((bf16[4,192,1024]{2,1,0:T(8,128)(2,1)}), bf16[4,192,1024]{2,1,0:T(8,128)(2,1)}, u32[]{:S(2)}, u32[]{:S(2)}) async-start(bf16[4,192,1024]{2,1,0:T(8,128)(2,1)} %bitcast.100), calls=%async_computation.3 | async-start | bytes 3145728 | tf_op jit(solution)/shard_map/all_to_all | solution.py:90
  270.3 2.1 fusion.54
  272.4 2.0 convolution_bitcast_fusion
  274.5 2.0 fusion.11
  277.6 28.0 %all-to-all-done.2 = bf16[4,192,1024]{2,1,0:T(8,128)(2,1)} async-done(((bf16[4,192,1024]{2,1,0:T(8,128)(2,1)}), bf16[4,192,1024]{2,1,0:T(8,128)(2,1)}, u32[]{:S(2)}, u32[]{:S(2)}) %all-to-all-start.2) | async-done | bytes 1572896 | tf_op jit(solution)/shard_map/all_to_all | solution.py:90
  305.7 4.2 %all-to-all-start.6 = ((bf16[4,64,1024]{2,1,0:T(8,128)(2,1)}), bf16[4,64,1024]{2,1,0:T(8,128)(2,1)}, u32[]{:S(2)}, u32[]{:S(2)}) async-start(bf16[4,64,1024]{2,1,0:T(8,128)(2,1)} %bitcast.93), calls=%async_computation.8 | async-start | bytes 1048576 | tf_op jit(solution)/shard_map/all_to_all | solution.py:99
  309.9 2.0 convolution_bitcast_fusion.2
  311.9 2.1 fusion.10
  315.2 3.6 %all-to-all-done.6 = bf16[4,64,1024]{2,1,0:T(8,128)(2,1)} async-done(((bf16[4,64,1024]{2,1,0:T(8,128)(2,1)}), bf16[4,64,1024]{2,1,0:T(8,128)(2,1)}, u32[]{:S(2)}, u32[]{:S(2)}) %all-to-all-start.6) | async-done | bytes 524320 | tf_op jit(solution)/shard_map/all_to_all | solution.py:99
  318.8 12.3 %all_to_all.37 = bf16[4,64,1024]{2,1,0:T(8,128)(2,1)S(1)} all-to-all(bf16[4,64,1024]{2,1,0:T(8,128)(2,1)} %bitcast.94), channel_id=1, replica_groups=mesh['grp'=2,'ep'=4,'dp'=4] {'dp'}, dimensions={0} | all-to-all | bytes 1048576 | tf_op jit(solution)/shard_map/all_to_all | solution.py:99
  (73 shorter events, 15.5 us)
Async XLA Ops:
  6.5 210.5 %copy-start = (bf16[1,1536,1024]{2,1,0:T(8,128)(2,1)S(1)}, bf16[1,1536,1024]{2,1,0:T(8,128)(2,1)}, u32[]{:S(2)}) copy-start(bf16[1,1536,1024]{2,1,0:T(8,128)(2,1)} %param.17) | copy-start | bytes 9437188
  9.3 8.4 %copy-start.3 = (f32[2,64,2]{1,2,0:T(2,128)S(1)}, f32[2,64,2]{1,2,0:T(2,128)}, u32[]{:S(2)}) copy-start(f32[2,64,2]{1,2,0:T(2,128)} %param.14) | copy-start | bytes 3076
  9.3 8.5 %copy-start.4 = (s32[2,64,2]{1,2,0:T(2,128)S(1)}, s32[2,64,2]{1,2,0:T(2,128)}, u32[]{:S(2)}) copy-start(s32[2,64,2]{1,2,0:T(2,128)} %param.13) | copy-start | bytes 3076
  11.9 28.7 %all-to-all-start = ((bf16[4,2,64,1024]{3,2,1,0:T(8,128)(2,1)}), bf16[4,2,64,1024]{3,2,1,0:T(8,128)(2,1)}, u32[]{:S(2)}, u32[]{:S(2)}) async-start(bf16[4,2,64,1024]{3,2,1,0:T(8,128)(2,1)} %copy.67), calls=%async_computation | async-start | bytes 2097152 | tf_op jit(solution)/shard_map/all_to_all | solution.py:36
  16.1 128.8 %reduce-scatter.5.cloned.1.call-start = ((), (), s32[]{:S(2)}) async-start(), calls=%async_computation.11 | async-start | bytes 5898240 | tf_op jit(solution)/shard_map/reduce_scatter | solution.py:83
  40.6 47.0 %copy-start.7 = (bf16[1,1024,1536]{2,1,0:T(8,128)(2,1)S(1)}, bf16[1,1024,1536]{2,1,0:T(8,128)(2,1)}, u32[]{:S(2)}) copy-start(bf16[1,1024,1536]{2,1,0:T(8,128)(2,1)} %param.15) | copy-start | bytes 9437188
  43.0 44.6 %copy-start.5 = (bf16[1,1024,1536]{2,1,0:T(8,128)(2,1)S(1)}, bf16[1,1024,1536]{2,1,0:T(8,128)(2,1)}, u32[]{:S(2)}) copy-start(bf16[1,1024,1536]{2,1,0:T(8,128)(2,1)} %param.16) | copy-start | bytes 9437188
  94.6 96.7 %reduce-scatter.3.cloned.1.call-start = ((), (), s32[]{:S(2)}) async-start(), calls=%async_computation.9 | async-start | bytes 5898240 | tf_op jit(solution)/shard_map/reduce_scatter | solution.py:83
  95.3 40.9 %copy-start.6 = (bf16[1,1024,1536]{2,1,0:T(8,128)(2,1)S(1)}, bf16[1,1024,1536]{2,1,0:T(8,128)(2,1)}, u32[]{:S(2)}) copy-start(bf16[1,1024,1536]{2,1,0:T(8,128)(2,1)} %param.16) | copy-start | bytes 9437188
  144.8 72.2 %all-gather.5.cloned.1.call-start = ((), (), s32[]{:S(2)}) async-start(), calls=%async_computation.12 | async-start | bytes 2949120 | tf_op jit(solution)/shard_map/all_gather | solution.py:87
  147.6 94.9 %all-gather.3.cloned.1.call-start = ((), (), s32[]{:S(2)}) async-start(), calls=%async_computation.10 | async-start | bytes 2949120 | tf_op jit(solution)/shard_map/all_gather | solution.py:87
  222.5 4.8 %copy-start.2 = (s32[2,1,8]{2,1,0:T(1,128)S(1)}, s32[2,1,8]{2,1,0:T(1,128)}, u32[]{:S(2)}) copy-start(s32[2,1,8]{2,1,0:T(1,128)} %param.12) | copy-start | bytes 196
  222.5 42.2 %all-to-all-start.5 = ((bf16[4,192,1024]{2,1,0:T(8,128)(2,1)}), bf16[4,192,1024]{2,1,0:T(8,128)(2,1)}, u32[]{:S(2)}, u32[]{:S(2)}) async-start(bf16[4,192,1024]{2,1,0:T(8,128)(2,1)} %bitcast.101), calls=%async_computation.7 | async-start | bytes 3145728 | tf_op jit(solution)/shard_map/all_to_all | solution.py:90
  264.7 41.0 %all-to-all-start.2 = ((bf16[4,192,1024]{2,1,0:T(8,128)(2,1)}), bf16[4,192,1024]{2,1,0:T(8,128)(2,1)}, u32[]{:S(2)}, u32[]{:S(2)}) async-start(bf16[4,192,1024]{2,1,0:T(8,128)(2,1)} %bitcast.100), calls=%async_computation.3 | async-start | bytes 3145728 | tf_op jit(solution)/shard_map/all_to_all | solution.py:90
  305.7 13.1 %all-to-all-start.6 = ((bf16[4,64,1024]{2,1,0:T(8,128)(2,1)}), bf16[4,64,1024]{2,1,0:T(8,128)(2,1)}, u32[]{:S(2)}, u32[]{:S(2)}) async-start(bf16[4,64,1024]{2,1,0:T(8,128)(2,1)} %bitcast.93), calls=%async_computation.8 | async-start | bytes 1048576 | tf_op jit(solution)/shard_map/all_to_all | solution.py:99
  311.9 2.1 copy-start.1
Sparse Core Ops, SparseCore 0:
  94.8 46.0 reduce-scatter.4
  145.0 46.3 reduce-scatter.2
  193.0 24.0 all-gather.4
  218.5 24.0 all-gather.2

commit v2 on v1

v2 whole, which is shorter than its diff:
```python
import functools

import jax
import jax.numpy as jnp
from jax import lax
from jax.experimental import pallas as pl
from jax.experimental.pallas import tpu as pltpu
from jax.sharding import PartitionSpec as P

SPANS = 2
UNITS = 4
TILE = 512


def dot32(left, right):
    return jnp.dot(left, right, preferred_element_type=jnp.float32)


def experts_kernel(
    ep_count,
    batches,
    outgoing,
    gate_hbm,
    up_hbm,
    down_hbm,
    returned,
    w_both,
    w_out,
    recv,
    parts,
    pair_in,
    cross_out,
    cross_in,
    hid,
    eo,
    w_sem,
    own_sem,
    z_send,
    z_recv,
    pair_send,
    pair_recv,
    cross_send,
    cross_recv,
    hop_send,
    hop_recv,
    fill_send,
    fill_recv,
    back_send,
    back_recv,
):
    me = lax.axis_index("ep")
    rank = lax.axis_index("dp")
    low, high = lax.rem(rank, 2), rank // 2
    pair = high * 2 + (1 - low)
    cross = (1 - high) * 2 + low
    slots = recv.shape[1]
    capacity = slots // ep_count
    unit = slots // UNITS
    half, quarter = unit // 2, unit // 4
    per_unit = ep_count // UNITS
    units = w_both.shape[1] // 2

    def rows_at(start, size):
        return pl.ds(pl.multiple_of(start, 16), size)

    def remote(src, dst, send, recv_sem, where):
        return pltpu.make_async_remote_copy(
            src_ref=src,
            dst_ref=dst,
            send_sem=send,
            recv_sem=recv_sem,
            device_id=where,
            device_id_type=pl.DeviceIdType.MESH,
        )

    def dispatch(m, s):
        target = lax.rem(me + s, ep_count)
        return remote(
            outgoing.at[m, rows_at(target * capacity, capacity)],
            recv.at[m, pl.ds(s * capacity, capacity)],
            z_send.at[m, s],
            z_recv.at[m, s],
            {"ep": target},
        )

    def give_back(m, s):
        target = lax.rem(me - s + ep_count, ep_count)
        return remote(
            eo.at[m, pl.ds(s * capacity, capacity)],
            returned.at[m, rows_at(me * capacity, capacity)],
            back_send.at[m, s],
            back_recv.at[m, s],
            {"ep": target},
        )

    def own_in(m):
        return pltpu.make_async_copy(
            outgoing.at[m, rows_at(me * capacity, capacity)], recv.at[m, pl.ds(0, capacity)], own_sem.at[m]
        )

    def own_back(m):
        return pltpu.make_async_copy(
            eo.at[m, pl.ds(0, capacity)], returned.at[m, rows_at(me * capacity, capacity)], own_sem.at[batches + m]
        )

    def pair_copy(m, u):
        k = m * UNITS + u
        return remote(
            parts.at[m, rows_at(u * unit + (1 - low) * half, half)],
            pair_in.at[k],
            pair_send.at[k],
            pair_recv.at[k],
            {"dp": pair},
        )

    def cross_copy(m, u):
        k = m * UNITS + u
        return remote(cross_out.at[k], cross_in.at[k], cross_send.at[k], cross_recv.at[k], {"dp": cross})

    def hop_copy(m, u):
        k = m * UNITS + u
        block = hid.at[m, rows_at(u * unit + low * half + high * quarter, quarter)]
        return remote(block, block, hop_send.at[k], hop_recv.at[k], {"dp": cross})

    def fill_copy(m, u):
        k = m * UNITS + u
        block = hid.at[m, rows_at(u * unit + low * half, half)]
        return remote(block, block, fill_send.at[k], fill_recv.at[k], {"dp": pair})

    weights = [
        pltpu.make_async_copy(gate_hbm, w_both.at[:, pl.ds(0, units)], w_sem.at[0]),
        pltpu.make_async_copy(up_hbm, w_both.at[:, pl.ds(units, units)], w_sem.at[1]),
        pltpu.make_async_copy(down_hbm, w_out, w_sem.at[2]),
    ]
    own_in(0).start()
    for copy in weights:
        copy.start()
    for m in range(1, batches):
        own_in(m).start()

    barrier = pltpu.get_barrier_semaphore()
    for s in range(1, ep_count):
        pl.semaphore_signal(
            barrier,
            inc=1,
            device_id={"ep": lax.rem(me + s, ep_count)},
            device_id_type=pl.DeviceIdType.MESH,
        )
    for peer in (pair, cross):
        pl.semaphore_signal(barrier, inc=1, device_id={"dp": peer}, device_id_type=pl.DeviceIdType.MESH)
    pl.semaphore_wait(barrier, ep_count + 1)

    for s in range(1, ep_count):
        dispatch(0, s).start()

    def columns(i):
        return pl.ds(pl.multiple_of(i * TILE, TILE), TILE)

    def project(m, u):
        for s in range(u * per_unit, (u + 1) * per_unit):
            if s == 0:
                own_in(m).wait()
            else:
                dispatch(m, s).wait_recv()
        if m == 0 and u == 0:
            weights[0].wait()
            weights[1].wait()
        rows = pl.ds(u * unit, unit)

        def tile(i, carry):
            parts[m, rows, columns(i)] = dot32(recv[m, rows, :], w_both[:, columns(i)]).astype(jnp.bfloat16)
            return carry

        lax.fori_loop(0, 2 * units // TILE, tile, 0)
        pair_copy(m, u).start()
        if u == 2 and m + 1 < batches:
            for s in range(1, ep_count):
                dispatch(m + 1, s).start()

    def add_pair(m, u):
        k = m * UNITS + u
        pair_copy(m, u).wait_recv()
        mine = rows_at(u * unit + low * half + (1 - high) * quarter, quarter)
        theirs = rows_at((1 - high) * quarter, quarter)

        def tile(i, carry):
            total = parts[m, mine, columns(i)].astype(jnp.float32) + pair_in[k, theirs, columns(i)].astype(jnp.float32)
            cross_out[k, :, columns(i)] = total.astype(jnp.bfloat16)
            return carry

        lax.fori_loop(0, 2 * units // TILE, tile, 0)
        cross_copy(m, u).start()

    def activate(m, u):
        k = m * UNITS + u
        cross_copy(m, u).wait_recv()
        mine = rows_at(u * unit + low * half + high * quarter, quarter)
        theirs = rows_at(high * quarter, quarter)

        def total(cols):
            return (
                parts[m, mine, cols].astype(jnp.float32)
                + pair_in[k, theirs, cols].astype(jnp.float32)
                + cross_in[k, :, cols].astype(jnp.float32)
            )

        def tile(i, carry):
            gate = total(columns(i))
            up = total(pl.ds(pl.multiple_of(units + i * TILE, TILE), TILE))
            hid[m, mine, columns(i)] = (jax.nn.silu(gate) * up).astype(jnp.bfloat16)
            return carry

        lax.fori_loop(0, units // TILE, tile, 0)
        hop_copy(m, u).start()

    def forward(m, u):
        hop_copy(m, u).wait_recv()
        fill_copy(m, u).start()

    def finish(m, u):
        fill_copy(m, u).wait_recv()
        if m == 0 and u == 0:
            weights[2].wait()
        rows = pl.ds(u * unit, unit)

        def tile(i, carry):
            eo[m, rows, columns(i)] = dot32(hid[m, rows, :], w_out[:, columns(i)]).astype(jnp.bfloat16)
            return carry

        lax.fori_loop(0, w_out.shape[1] // TILE, tile, 0)
        for s in range(u * per_unit, (u + 1) * per_unit):
            if s == 0:
                own_back(m).start()
            else:
                give_back(m, s).start()

    steps = [(m, u) for m in range(batches) for u in range(UNITS)]
    stages = (project, add_pair, activate, forward, finish)
    for step in range(len(steps) + len(stages) - 1):
        for lag, stage in enumerate(stages):
            if 0 <= step - lag < len(steps):
                stage(*steps[step - lag])

    for m, u in steps:
        pair_copy(m, u).wait_send()
        cross_copy(m, u).wait_send()
        hop_copy(m, u).wait_send()
        fill_copy(m, u).wait_send()
    for m in range(batches):
        own_back(m).wait()
        for s in range(1, ep_count):
            dispatch(m, s).wait_send()
            give_back(m, s).wait_send()
            back_from = lax.rem(me + s, ep_count)
            remote(
                eo.at[m, pl.ds(s * capacity, capacity)],
                returned.at[m, rows_at(back_from * capacity, capacity)],
                back_send.at[m, s],
                back_recv.at[m, s],
                {"ep": back_from},
            ).wait_recv()


def run_experts(outgoing, gate, up, down, ep_count):
    batches, slots, feat = outgoing.shape
    units = gate.shape[1]
    count = batches * UNITS
    unit = slots // UNITS
    half, quarter = unit // 2, unit // 4
    bf16 = jnp.bfloat16
    dma = pltpu.SemaphoreType.DMA
    return pl.pallas_call(
        functools.partial(experts_kernel, ep_count, batches),
        out_shape=jax.ShapeDtypeStruct((batches, slots, feat), bf16),
        in_specs=[pl.BlockSpec(memory_space=pl.ANY)] * 4,
        out_specs=pl.BlockSpec(memory_space=pl.ANY),
        scratch_shapes=[
            pltpu.VMEM((feat, 2 * units), bf16),
            pltpu.VMEM((units, feat), bf16),
            pltpu.VMEM((batches, slots, feat), bf16),
            pltpu.VMEM((batches, slots, 2 * units), bf16),
            pltpu.VMEM((count, half, 2 * units), bf16),
            pltpu.VMEM((count, quarter, 2 * units), bf16),
            pltpu.VMEM((count, quarter, 2 * units), bf16),
            pltpu.VMEM((batches, slots, units), bf16),
            pltpu.VMEM((batches, slots, feat), bf16),
            dma((3,)),
            dma((2 * batches,)),
            dma((batches, ep_count)),
            dma((batches, ep_count)),
            dma((count,)),
            dma((count,)),
            dma((count,)),
            dma((count,)),
            dma((count,)),
            dma((count,)),
            dma((count,)),
            dma((count,)),
            dma((batches, ep_count)),
            dma((batches, ep_count)),
        ],
        compiler_params=pltpu.CompilerParams(
            collective_id=0, has_side_effects=True, vmem_limit_bytes=60 * 1024 * 1024
        ),
        cost_estimate=pl.CostEstimate(
            flops=6 * batches * slots * feat * units, bytes_accessed=20 * 2**20, transcendentals=batches * slots * units
        ),
    )(outgoing, gate, up, down)


def local(hidden_in, norm_gain, span_plan, route_ids, route_gates, w_gate, w_up, w_down):
    dp_count = lax.axis_size("dp")
    ep_count = lax.axis_size("ep")
    dp_rank = lax.axis_index("dp")
    batches, tok_rows, width = hidden_in.shape
    routes = route_ids.shape[2]
    span_rows = tok_rows // SPANS
    group_rows = dp_count * tok_rows
    feat = width // dp_count
    capacity = -(-3 * group_rows * routes // (2 * ep_count) // 16) * 16
    slot_count = ep_count * capacity

    split = hidden_in.reshape(batches, tok_rows, dp_count, feat).transpose(2, 0, 1, 3)
    values = lax.all_to_all(split, "dp", split_axis=0, concat_axis=0, tiled=True)
    rows = values.transpose(1, 0, 2, 3).reshape(batches, group_rows, feat)
    wide = hidden_in.astype(jnp.float32)
    factor = lax.rsqrt(jnp.mean(wide * wide, -1, keepdims=True) + 1e-06)
    facts = jnp.concatenate([factor, route_ids.astype(jnp.float32), route_gates], -1)
    facts = lax.all_gather(facts, "dp", axis=1, tiled=True)
    ids = facts[:, :, 1 : 1 + routes, None]
    gates = facts[:, :, 1 + routes :, None]
    gain = lax.dynamic_slice_in_dim(norm_gain, dp_rank * feat, feat, 0).astype(jnp.float32)

    experts = jnp.arange(ep_count, dtype=jnp.float32)
    slot_place = jnp.arange(capacity, dtype=jnp.float32)
    chosen = ids == experts
    named = jnp.sum(chosen.astype(jnp.float32), 2)
    weight = jnp.sum(jnp.where(chosen, gates, 0.0), 2)
    numbers = jnp.arange(group_rows)
    earlier = (numbers[:, None] > numbers[None, :]).astype(jnp.bfloat16)
    place = jnp.einsum("ts,mse->mte", earlier, named.astype(jnp.bfloat16), preferred_element_type=jnp.float32)
    where = jnp.where(named > 0, place, -1.0)
    pick = (where.transpose(0, 2, 1)[:, :, None, :] == slot_place[None, None, :, None]).astype(jnp.bfloat16)
    pick = pick.reshape(batches, slot_count, group_rows)
    normed = (rows.astype(jnp.float32) * facts[:, :, :1] * gain).astype(jnp.bfloat16)
    outgoing = jnp.einsum("mst,mtf->msf", pick, normed, preferred_element_type=jnp.float32).astype(jnp.bfloat16)

    plan = span_plan[:, 0]
    table = jnp.concatenate([where, weight], 2).reshape(batches, -1, span_rows, 2 * ep_count)
    table = jnp.take_along_axis(table, plan[:, :, None, None], axis=1).reshape(batches, group_rows, 2 * ep_count)
    spread = jnp.where(
        table[:, :, :ep_count, None] == slot_place, table[:, :, ep_count:, None], 0.0
    ).reshape(batches, group_rows, slot_count)
    high = spread.astype(jnp.bfloat16)
    low = (spread - high.astype(jnp.float32)).astype(jnp.bfloat16)
    source = (plan[:, :, None] * span_rows + jnp.arange(span_rows)).reshape(batches, group_rows)
    order = (source[:, :, None] == numbers).astype(jnp.bfloat16)

    returned = run_experts(outgoing, w_gate[0], w_up[0], w_down[0], ep_count)

    def mix(left, right):
        return jnp.einsum("mts,msf->mtf", left, right, preferred_element_type=jnp.float32)

    total = mix(high, returned) + mix(low, returned) + mix(order, rows)
    combined = total.astype(jnp.bfloat16).reshape(batches, dp_count, tok_rows, feat).transpose(1, 0, 2, 3)
    outputs = lax.all_to_all(combined, "dp", split_axis=0, concat_axis=0, tiled=True)
    return outputs.transpose(1, 2, 0, 3).reshape(batches, tok_rows, width)


def solution(mesh):
    return jax.shard_map(
        local,
        mesh=mesh,
        in_specs=(
            P(None, ("grp", "ep", "dp"), None),
            P(),
            P(None, ("grp", "ep"), None),
            P(None, ("grp", "ep", "dp"), None),
            P(None, ("grp", "ep", "dp"), None),
            P("ep", "dp", None),
            P("ep", "dp", None),
            P("ep", None, "dp"),
        ),
        out_specs=P(None, ("grp", "ep", "dp"), None),
        check_vma=False,
    )
```

time: 341 us -> 206 us (0.60)
  Pallas kernels: 0 us -> 151 us
  waiting for transfers between devices: 129 us -> 0.01 us
  blocking collectives: 109 us -> 33.1 us
  matrix products: 41.3 us -> 7.6 us
  starting transfers between devices: 17.8 us -> 4.34 us
  between operations: 13.4 us -> 0.26 us
  other arithmetic: 12.7 us -> 2.92 us
  local copies, waits for them, and re-layouts: 15.6 us -> 7.07 us
    pallas_call x0 -> x1, Pallas kernels: none -> 151 us  [run_experts(): pl.pallas_call(functools.partial(experts_kernel, ep_count, batches), out_...]
    all_to_all x2 -> x0, blocking collectives: 82.1 us -> none  [local(): lax.all_to_all(outgoing.reshape(ep_count, capacity, feat), 'ep', split_ax...]
    all_to_all x3 -> x0, waiting for transfers between devices: 48.4 us -> none  [the longest x2 44.8 us: local(): lax.all_to_all(expert_out.reshape(ep_count, capacity, feat), 'ep', split_...]
    reduce_scatter x2 -> x0, waiting for transfers between devices: 43.5 us -> none  [local(): lax.psum_scatter(parts, 'dp', scatter_dimension=0, tiled=True)]
    all_gather x2 -> x0, waiting for transfers between devices: 37.5 us -> none  [local(): hidden = lax.all_gather(hidden, 'dp', axis=0, tiled=True)]
    dot_general x14 -> x5, matrix products: 41.3 us -> 7.6 us  [the longest x3 4.66 us: mix(): jnp.einsum('mts,msf->mtf', left, right, preferred_element_type=jnp.float32)]
    all_to_all x3 -> x0, starting transfers between devices: 13.2 us -> none  [the longest x2 9.08 us: local(): lax.all_to_all(expert_out.reshape(ep_count, capacity, feat), 'ep', split_...]
    convert_element_type x5 -> x2, other arithmetic: 7.77 us -> 1.31 us  [the longest x1 1.12 us: local(): low = (spread - high.astype(jnp.float32)).astype(jnp.bfloat16)]
  transfers between devices with their start and end apart: 8 -> 1, of which waited for: 6 -> 0; matrix products, arithmetic and copies ran while one was open for 15% -> 3% of each run, Pallas kernels for 0% -> 0%
where the time goes in v2:
time: 206 us
  Pallas kernels  151 us (73%)
  blocking collectives  33.1 us (16%)
  matrix products  7.6 us (4%)
  local copies, waits for them, and re-layouts  7.07 us (3%)
  starting transfers between devices  4.34 us (2%)
  other arithmetic  2.92 us (1%)
    pallas_call x1, Pallas kernels, run_experts(): pl.pallas_call(functools.partial(experts_kernel, ep_count, batches), out_...  151 us
    all_to_all x1, blocking collectives, local(): lax.all_to_all(combined, 'dp', split_axis=0, concat_axis=0, tiled=True)  17.3 us
    all_gather x1, blocking collectives, local(): facts = lax.all_gather(facts, 'dp', axis=1, tiled=True)  15.8 us
    dot_general x3, matrix products, mix(): jnp.einsum('mts,msf->mtf', left, right, preferred_element_type=jnp.float32)  4.66 us
    all_to_all x1, starting transfers between devices, local(): lax.all_to_all(split, 'dp', split_axis=0, concat_axis=0, tiled=True)  4.34 us
  transfers between devices with their start and end apart: 1, of which 0 were waited for; matrix products, arithmetic and copies ran while one was open for 3% of the time, Pallas kernels for 0%

profile of v2, /device:TPU:0, one launch (start us, length us, event | category | flops | bytes accessed | tf_op | source)
XLA Modules:
  0.0 206.1 jit_solution(12842842995891134361)
XLA Ops:
  0.0 1.8 reshape.139
  1.9 1.3 copy.90
  3.2 4.3 %all-to-all-start = ((bf16[4,2,64,1024]{3,2,1,0:T(8,128)(2,1)}), bf16[4,2,64,1024]{3,2,1,0:T(8,128)(2,1)S(1)}, u32[]{:S(2)}, u32[]{:S(2)}) async-start(bf16[4,2,64,1024]{3,2,1,0:T(8,128)(2,1)} %copy.90), calls=%async_computation | async-start | bytes 2097152 | tf_op jit(solution)/shard_map/all_to_all | solution.py:324
  7.5 0.3 multiply_reduce_fusion
  7.8 0.1 copy.81
  8.0 0.1 copy.82
  8.1 0.1 copy.83
  8.2 0.2 pad_maximum_fusion
  8.4 15.8 %all_gather.3 = f32[2,256,5]{2,0,1:T(2,128)S(1)} all-gather(f32[2,64,5]{2,0,1:T(2,128)S(1)} %pad_maximum_fusion), channel_id=1, replica_groups=mesh['grp'=2,'ep'=4,'dp'=4] {'dp'}, dimensions={1}, use_global_device_ids=true | all-gather | bytes 12800 | tf_op jit(solution)/shard_map/all_gather | solution.py:329
  24.2 0.6 fusion.13
  24.8 0.1 copy.84
  24.9 0.1 copy.85
  25.1 0.2 bitcast_select_fusion.2
  25.4 0.1 reshape.143
  25.5 0.6 gather_fusion
  26.1 0.1 gather.7
  26.3 0.1 broadcast_in_dim.59
  26.6 1.1 fusion.2
  27.7 0.2 fusion.1
  27.9 0.3 bitcast_compare_fusion
  28.2 0.1 copy.92
  28.4 0.1 add.75
  28.5 0.1 add.77
  28.5 0.7 dynamic-slice_convert_fusion
  29.2 0.1 copy.91
  29.4 2.8 %convolution_convert_fusion.outgoing = bf16[2,768,1024]{2,1,0:T(8,128)(2,1)} fusion(pred[2,768,256]{2,1,0:T(32,128)(4,1)S(1)} %bitcast_compare_fusion, bf16[2,256,1024]{2,1,0:T(8,128)(2,1)S(1)} %bitcast.60, f32[1024]{0:T(1024)S(1)} %dynamic-slice_convert_fusion, f32[2,256]{1,0:T(2,128)S(1)} %bitcast.68), kind=kOutput, calls=%fused_computation.1 | convolution fusion | flops 808976384 | bytes 4593664 | tf_op jit(solution)/shard_map/mst,mtf->msf/dot_general | solution.py:346
  32.1 150.8 %shard_map.82 = bf16[2,768,1024]{2,1,0:T(8,128)(2,1)} custom-call(bf16[2,768,1024]{2,1,0:T(8,128)(2,1)} %convolution_convert_fusion.outgoing, bf16[1024,1536]{1,0:T(8,128)(2,1)} %bitcast.72, bf16[1024,1536]{1,0:T(8,128)(2,1)} %bitcast.73, bf16[1536,1024]{1,0:T(8,128)(2,1)} %bitcast.74), custom_call_target="tpu_custom_call" | custom-call | flops 14495514624 | bytes 20971520 | tf_op jit(solution)/shard_map/pallas_call | solution.py:272
  183.0 3.1 %fusion.16 = f32[2,256,1024]{2,1,0:T(8,128)S(1)} fusion(bf16[2,256,768]{1,2,0:T(8,128)(2,1)S(1)} %copy-done.2, bf16[2,768,1024]{2,1,0:T(8,128)(2,1)} %shard_map.82), kind=kOutput, calls=%fused_computation.42 | convolution fusion | flops 805306368 | bytes 6029312 | tf_op jit(solution)/shard_map/mts,msf->mtf/dot_general | solution.py:362
  186.0 1.0 fusion.15
  187.1 0.6 add_convert_fusion
  187.7 17.3 %all_to_all.10 = bf16[4,2,64,1024]{3,2,1,0:T(8,128)(2,1)S(1)} all-to-all(bf16[4,2,64,1024]{3,2,1,0:T(8,128)(2,1)S(1)} %bitcast.64), channel_id=1, replica_groups=mesh['grp'=2,'ep'=4,'dp'=4] {'dp'}, dimensions={0} | all-to-all | bytes 2097152 | tf_op jit(solution)/shard_map/all_to_all | solution.py:366
  205.0 1.1 copy.99
  (35 shorter events, 0.6 us)
Async XLA Ops:
  1.9 5.6 %copy-start.1 = (bf16[2,64,4096]{2,1,0:T(8,128)(2,1)S(1)}, bf16[2,64,4096]{2,1,0:T(8,128)(2,1)}, u32[]{:S(2)}) copy-start(bf16[2,64,4096]{2,1,0:T(8,128)(2,1)} %param.8) | copy-start | bytes 3145732
  3.1 4.8 %copy-start.5 = (s32[2,64,2]{1,2,0:T(2,128)S(1)}, s32[2,64,2]{1,2,0:T(2,128)}, u32[]{:S(2)}) copy-start(s32[2,64,2]{1,2,0:T(2,128)} %param.11) | copy-start | bytes 3076
  3.2 4.9 %copy-start.4 = (f32[2,64,2]{1,2,0:T(2,128)S(1)}, f32[2,64,2]{1,2,0:T(2,128)}, u32[]{:S(2)}) copy-start(f32[2,64,2]{1,2,0:T(2,128)} %param.12) | copy-start | bytes 3076
  3.2 26.1 %all-to-all-start = ((bf16[4,2,64,1024]{3,2,1,0:T(8,128)(2,1)}), bf16[4,2,64,1024]{3,2,1,0:T(8,128)(2,1)S(1)}, u32[]{:S(2)}, u32[]{:S(2)}) async-start(bf16[4,2,64,1024]{3,2,1,0:T(8,128)(2,1)} %copy.90), calls=%async_computation | async-start | bytes 2097152 | tf_op jit(solution)/shard_map/all_to_all | solution.py:324
  7.5 17.9 %copy-start.3 = (s32[2,1,8]{2,1,0:T(1,128)S(1)}, s32[2,1,8]{2,1,0:T(1,128)}, u32[]{:S(2)}) copy-start(s32[2,1,8]{2,1,0:T(1,128)} %param.10) | copy-start | bytes 196
  32.1 150.8 %copy-start.2 = (bf16[2,256,768]{1,2,0:T(8,128)(2,1)S(1)}, bf16[2,256,768]{1,2,0:T(8,128)(2,1)}, u32[]{:S(2)}) copy-start(bf16[2,256,768]{1,2,0:T(8,128)(2,1)} %fusion.2) | copy-start | bytes 2359300
  183.0 3.1 %copy-start = (bf16[2,768,1024]{2,1,0:T(8,128)(2,1)S(1)}, bf16[2,768,1024]{2,1,0:T(8,128)(2,1)}, u32[]{:S(2)}) copy-start(bf16[2,768,1024]{2,1,0:T(8,128)(2,1)} %shard_map.82) | copy-start | bytes 9437188

commit v3 on v2

--- a/solution.py
+++ b/solution.py
@@ -19,17 +19,25 @@
 def experts_kernel(
     ep_count,
     batches,
-    outgoing,
+    tokens,
+    pick,
+    factor,
+    gain,
+    mix_high,
+    mix_low,
+    order,
     gate_hbm,
     up_hbm,
     down_hbm,
-    returned,
+    mixed,
     w_both,
     w_out,
+    rows_in,
+    outgoing,
+    returned,
     recv,
     parts,
     pair_in,
-    cross_out,
     cross_in,
     hid,
     eo,
@@ -47,6 +55,11 @@
     fill_recv,
     back_send,
     back_recv,
+    in_send,
+    in_recv,
+    out_send,
+    out_recv,
+    edge_sem,
 ):
     me = lax.axis_index("ep")
     rank = lax.axis_index("dp")
@@ -59,6 +72,10 @@
     half, quarter = unit // 2, unit // 4
     per_unit = ep_count // UNITS
     units = w_both.shape[1] // 2
+    tok_rows = tokens.shape[1]
+    feat = rows_in.shape[2]
+    across = (1 - high) * 2 + (1 - low)
+    peers = (across, cross, pair)
 
     def rows_at(start, size):
         return pl.ds(pl.multiple_of(start, 16), size)
@@ -93,6 +110,39 @@
             {"ep": target},
         )
 
+    def feats_at(owner):
+        return pl.ds(pl.multiple_of(owner * feat, 128), feat)
+
+    def slice_out(m, p):
+        return remote(
+            tokens.at[m, :, feats_at(peers[p])],
+            rows_in.at[m, rows_at(rank * tok_rows, tok_rows)],
+            in_send.at[m, p],
+            in_recv.at[m, p],
+            {"dp": peers[p]},
+        )
+
+    def own_slice(m):
+        return pltpu.make_async_copy(
+            tokens.at[m, :, feats_at(rank)], rows_in.at[m, rows_at(rank * tok_rows, tok_rows)], edge_sem.at[m]
+        )
+
+    def row_back(m, p):
+        return remote(
+            rows_in.at[m, rows_at(peers[p] * tok_rows, tok_rows)],
+            mixed.at[m, :, feats_at(rank)],
+            out_send.at[m, p],
+            out_recv.at[m, p],
+            {"dp": peers[p]},
+        )
+
+    def own_row_back(m):
+        return pltpu.make_async_copy(
+            rows_in.at[m, rows_at(rank * tok_rows, tok_rows)],
+            mixed.at[m, :, feats_at(rank)],
+            edge_sem.at[batches + m],
+        )
+
     def own_in(m):
         return pltpu.make_async_copy(
             outgoing.at[m, rows_at(me * capacity, capacity)], recv.at[m, pl.ds(0, capacity)], own_sem.at[m]
@@ -115,7 +165,7 @@
 
     def cross_copy(m, u):
         k = m * UNITS + u
-        return remote(cross_out.at[k], cross_in.at[k], cross_send.at[k], cross_recv.at[k], {"dp": cross})
+        return remote(pair_in.at[k, rows_at((1 - high) * quarter, quarter)], cross_in.at[k], cross_send.at[k], cross_recv.at[k], {"dp": cross})
 
     def hop_copy(m, u):
         k = m * UNITS + u
@@ -132,11 +182,8 @@
         pltpu.make_async_copy(up_hbm, w_both.at[:, pl.ds(units, units)], w_sem.at[1]),
         pltpu.make_async_copy(down_hbm, w_out, w_sem.at[2]),
     ]
-    own_in(0).start()
-    for copy in weights:
-        copy.start()
-    for m in range(1, batches):
-        own_in(m).start()
+    for m in range(batches):
+        own_slice(m).start()
 
     barrier = pltpu.get_barrier_semaphore()
     for s in range(1, ep_count):
@@ -146,15 +193,61 @@
             device_id={"ep": lax.rem(me + s, ep_count)},
             device_id_type=pl.DeviceIdType.MESH,
         )
-    for peer in (pair, cross):
+    for peer in peers:
         pl.semaphore_signal(barrier, inc=1, device_id={"dp": peer}, device_id_type=pl.DeviceIdType.MESH)
-    pl.semaphore_wait(barrier, ep_count + 1)
-
+    pl.semaphore_wait(barrier, ep_count + 2)
+
+    for m in range(batches):
+        for p in range(len(peers)):
+            slice_out(m, p).start()
+    for copy in weights:
+        copy.start()
+
+    def columns(i):
+        return pl.ds(pl.multiple_of(i * TILE, TILE), TILE)
+
+    def prepare(m):
+        own_slice(m).wait()
+        for p in range(len(peers)):
+            slice_out(m, p).wait_recv()
+
+        def tile(i, carry):
+            wide = rows_in[m, :, columns(i)].astype(jnp.float32)
+            normed = (wide * factor[m] * gain[:, columns(i)]).astype(jnp.bfloat16)
+            outgoing[m, :, columns(i)] = dot32(pick[m], normed).astype(jnp.bfloat16)
+            return carry
+
+        lax.fori_loop(0, feat // TILE, tile, 0)
+        own_in(m).start()
+
+    def combine(m):
+        own_back(m).wait()
+        for s in range(1, ep_count):
+            back_from = lax.rem(me + s, ep_count)
+            remote(
+                eo.at[m, pl.ds(s * capacity, capacity)],
+                returned.at[m, rows_at(back_from * capacity, capacity)],
+                back_send.at[m, s],
+                back_recv.at[m, s],
+                {"ep": back_from},
+            ).wait_recv()
+
+        def tile(i, carry):
+            back = returned[m, :, columns(i)]
+            total = dot32(mix_high[m], back) + dot32(mix_low[m], back) + dot32(order[m], rows_in[m, :, columns(i)])
+            rows_in[m, :, columns(i)] = total.astype(jnp.bfloat16)
+            return carry
+
+        lax.fori_loop(0, feat // TILE, tile, 0)
+        for p in range(len(peers)):
+            row_back(m, p).start()
+        own_row_back(m).start()
+
+    prepare(0)
     for s in range(1, ep_count):
         dispatch(0, s).start()
-
-    def columns(i):
-        return pl.ds(pl.multiple_of(i * TILE, TILE), TILE)
+    for m in range(1, batches):
+        prepare(m)
 
     def project(m, u):
         for s in range(u * per_unit, (u + 1) * per_unit):
@@ -185,7 +278,7 @@
 
         def tile(i, carry):
             total = parts[m, mine, columns(i)].astype(jnp.float32) + pair_in[k, theirs, columns(i)].astype(jnp.float32)
-            cross_out[k, :, columns(i)] = total.astype(jnp.bfloat16)
+            pair_in[k, theirs, columns(i)] = total.astype(jnp.bfloat16)
             return carry
 
         lax.fori_loop(0, 2 * units // TILE, tile, 0)
@@ -241,28 +334,33 @@
             if 0 <= step - lag < len(steps):
                 stage(*steps[step - lag])
 
+    for m in range(batches):
+        combine(m)
     for m, u in steps:
         pair_copy(m, u).wait_send()
         cross_copy(m, u).wait_send()
         hop_copy(m, u).wait_send()
         fill_copy(m, u).wait_send()
     for m in range(batches):
-        own_back(m).wait()
         for s in range(1, ep_count):
             dispatch(m, s).wait_send()
             give_back(m, s).wait_send()
-            back_from = lax.rem(me + s, ep_count)
+        own_row_back(m).wait()
+        for p in range(len(peers)):
+            slice_out(m, p).wait_send()
+            row_back(m, p).wait_send()
             remote(
-                eo.at[m, pl.ds(s * capacity, capacity)],
-                returned.at[m, rows_at(back_from * capacity, capacity)],
-                back_send.at[m, s],
-                back_recv.at[m, s],
-                {"ep": back_from},
+                rows_in.at[m, rows_at(peers[p] * tok_rows, tok_rows)],
+                mixed.at[m, :, feats_at(peers[p])],
+                out_send.at[m, p],
+                out_recv.at[m, p],
+                {"dp": peers[p]},
             ).wait_recv()
 
 
-def run_experts(outgoing, gate, up, down, ep_count):
-    batches, slots, feat = outgoing.shape
+def run_experts(tokens, pick, factor, gain, mixers, gate, up, down, ep_count):
+    batches, slots, group_rows = pick.shape
+    feat = down.shape[1]
     units = gate.shape[1]
     count = batches * UNITS
     unit = slots // UNITS
@@ -271,16 +369,20 @@
     dma = pltpu.SemaphoreType.DMA
     return pl.pallas_call(
         functools.partial(experts_kernel, ep_count, batches),
-        out_shape=jax.ShapeDtypeStruct((batches, slots, feat), bf16),
-        in_specs=[pl.BlockSpec(memory_space=pl.ANY)] * 4,
+        out_shape=jax.ShapeDtypeStruct(tokens.shape, bf16),
+        in_specs=[pl.BlockSpec(memory_space=pl.ANY)]
+        + [pl.BlockSpec(memory_space=pltpu.VMEM)] * 6
+        + [pl.BlockSpec(memory_space=pl.ANY)] * 3,
         out_specs=pl.BlockSpec(memory_space=pl.ANY),
         scratch_shapes=[
             pltpu.VMEM((feat, 2 * units), bf16),
             pltpu.VMEM((units, feat), bf16),
+            pltpu.VMEM((batches, group_rows, feat), bf16),
+            pltpu.VMEM((batches, slots, feat), bf16),
+            pltpu.VMEM((batches, slots, feat), bf16),
             pltpu.VMEM((batches, slots, feat), bf16),
             pltpu.VMEM((batches, slots, 2 * units), bf16),
             pltpu.VMEM((count, half, 2 * units), bf16),
-            pltpu.VMEM((count, quarter, 2 * units), bf16),
             pltpu.VMEM((count, quarter, 2 * units), bf16),
             pltpu.VMEM((batches, slots, units), bf16),
             pltpu.VMEM((batches, slots, feat), bf16),
@@ -298,6 +400,11 @@
             dma((count,)),
             dma((batches, ep_count)),
             dma((batches, ep_count)),
+            dma((batches, 3)),
+            dma((batches, 3)),
+            dma((batches, 3)),
+            dma((batches, 3)),
+            dma((2 * batches,)),
         ],
         compiler_params=pltpu.CompilerParams(
             collective_id=0, has_side_effects=True, vmem_limit_bytes=60 * 1024 * 1024
@@ -305,7 +412,7 @@
         cost_estimate=pl.CostEstimate(
             flops=6 * batches * slots * feat * units, bytes_accessed=20 * 2**20, transcendentals=batches * slots * units
         ),
-    )(outgoing, gate, up, down)
+    )(tokens, pick, factor, gain, *mixers, gate, up, down)
 
 
 def local(hidden_in, norm_gain, span_plan, route_ids, route_gates, w_gate, w_up, w_down):
@@ -320,9 +427,6 @@
     capacity = -(-3 * group_rows * routes // (2 * ep_count) // 16) * 16
     slot_count = ep_count * capacity
 
-    split = hidden_in.reshape(batches, tok_rows, dp_count, feat).transpose(2, 0, 1, 3)
-    values = lax.all_to_all(split, "dp", split_axis=0, concat_axis=0, tiled=True)
-    rows = values.transpose(1, 0, 2, 3).reshape(batches, group_rows, feat)
     wide = hidden_in.astype(jnp.float32)
     factor = lax.rsqrt(jnp.mean(wide * wide, -1, keepdims=True) + 1e-06)
     facts = jnp.concatenate([factor, route_ids.astype(jnp.float32), route_gates], -1)
@@ -342,9 +446,6 @@
     where = jnp.where(named > 0, place, -1.0)
     pick = (where.transpose(0, 2, 1)[:, :, None, :] == slot_place[None, None, :, None]).astype(jnp.bfloat16)
     pick = pick.reshape(batches, slot_count, group_rows)
-    normed = (rows.astype(jnp.float32) * facts[:, :, :1] * gain).astype(jnp.bfloat16)
-    outgoing = jnp.einsum("mst,mtf->msf", pick, normed, preferred_element_type=jnp.float32).astype(jnp.bfloat16)
-
     plan = span_plan[:, 0]
     table = jnp.concatenate([where, weight], 2).reshape(batches, -1, span_rows, 2 * ep_count)
     table = jnp.take_along_axis(table, plan[:, :, None, None], axis=1).reshape(batches, group_rows, 2 * ep_count)
@@ -356,15 +457,17 @@
     source = (plan[:, :, None] * span_rows + jnp.arange(span_rows)).reshape(batches, group_rows)
     order = (source[:, :, None] == numbers).astype(jnp.bfloat16)
 
-    returned = run_experts(outgoing, w_gate[0], w_up[0], w_down[0], ep_count)
-
-    def mix(left, right):
-        return jnp.einsum("mts,msf->mtf", left, right, preferred_element_type=jnp.float32)
-
-    total = mix(high, returned) + mix(low, returned) + mix(order, rows)
-    combined = total.astype(jnp.bfloat16).reshape(batches, dp_count, tok_rows, feat).transpose(1, 0, 2, 3)
-    outputs = lax.all_to_all(combined, "dp", split_axis=0, concat_axis=0, tiled=True)
-    return outputs.transpose(1, 2, 0, 3).reshape(batches, tok_rows, width)
+    return run_experts(
+        hidden_in,
+        pick,
+        facts[:, :, :1],
+        gain[None, :],
+        (high, low, order),
+        w_gate[0],
+        w_up[0],
+        w_down[0],
+        ep_count,
+    )
 
 
 def solution(mesh):

time: 206 us -> 198 us (0.961)
  blocking collectives: 33.1 us -> 7.19 us
  Pallas kernels: 151 us -> 173 us
  matrix products: 7.6 us -> 0.17 us
  other arithmetic: 2.92 us -> 7.85 us
  starting transfers between devices: 4.34 us -> 0 us
    pallas_call x1, Pallas kernels: 151 us -> 173 us  [run_experts(): pl.pallas_call(functools.partial(experts_kernel, ep_count, batches), out_...]
    all_to_all x1 -> x0, blocking collectives: 17.3 us -> none  [local(): lax.all_to_all(combined, 'dp', split_axis=0, concat_axis=0, tiled=True)]
    all_gather x1, blocking collectives: 15.8 us -> 7.19 us  [local(): facts = lax.all_gather(facts, 'dp', axis=1, tiled=True)]
    dot_general x4 -> x0, matrix products: 7.43 us -> none  [the longest x3 4.66 us: mix(): jnp.einsum('mts,msf->mtf', left, right, preferred_element_type=jnp.float32)]
    all_to_all x1 -> x0, starting transfers between devices: 4.34 us -> none  [local(): lax.all_to_all(split, 'dp', split_axis=0, concat_axis=0, tiled=True)]
    broadcast_in_dim x0 -> x2, local copies, waits for them, and re-layouts: none -> 3.14 us  [local(): jnp.where(table[:, :, :ep_count, None] == slot_place, table[:, :, ep_coun...]
    reshape x3 -> x0, local copies, waits for them, and re-layouts: 2.98 us -> none  [the longest x1 1.85 us: local(): hidden_in.reshape(batches, tok_rows, dp_count, feat).transpose(2, 0, 1, 3)]
    unnamed x13 -> x6, local copies, waits for them, and re-layouts: 0.14 us -> 3.08 us
  transfers between devices with their start and end apart: 1 -> 0, of which waited for: 0 -> 0; matrix products, arithmetic and copies ran while one was open for 3% -> 0% of each run, Pallas kernels for 0% -> 0%
where the time goes in v3:
time: 198 us
  Pallas kernels  173 us (87%)
  local copies, waits for them, and re-layouts  8.82 us (4%)
  other arithmetic  7.85 us (4%)
  blocking collectives  7.19 us (4%)
    pallas_call x1, Pallas kernels, run_experts(): pl.pallas_call(functools.partial(experts_kernel, ep_count, batches), out_...  173 us
    all_gather x1, blocking collectives, local(): facts = lax.all_gather(facts, 'dp', axis=1, tiled=True)  7.19 us

profile of v3, /device:TPU:0, one launch (start us, length us, event | category | flops | bytes accessed | tf_op | source)
XLA Modules:
  0.0 197.7 jit_solution(7150073142579222510)
XLA Ops:
  0.0 1.5 multiply_reduce_fusion
  1.5 0.1 copy.37
  1.6 0.7 convert_element_type.31
  2.3 0.1 copy.38
  2.4 0.8 copy.39
  3.2 0.1 pad_maximum_fusion
  3.3 7.2 %all_gather.3 = f32[2,256,5]{2,1,0:T(8,128)S(1)} all-gather(f32[2,64,5]{2,1,0:T(8,128)S(1)} %pad_maximum_fusion), channel_id=1, replica_groups=mesh['grp'=2,'ep'=4,'dp'=4] {'dp'}, dimensions={1}, use_global_device_ids=true | all-gather | bytes 12800 | tf_op jit(solution)/shard_map/all_gather | solution.py:433
  10.5 0.2 fusion.10
  10.7 0.1 copy.40
  10.9 0.1 copy.41
  11.0 0.2 bitcast_select_fusion
  11.2 0.1 reshape.125
  11.3 0.1 reshape.127
  11.4 0.6 gather_fusion
  12.1 0.1 gather.7
  12.2 0.1 broadcast_in_dim.65
  12.2 0.1 broadcast_in_dim.66
  12.4 0.1 eq.75
  12.5 0.5 copy.45
  13.0 1.3 broadcast_in_dim.72
  14.3 1.9 copy.47
  16.1 0.1 eq.72
  16.2 1.1 subtract_convert_fusion.mix_low
  17.3 1.1 fusion.1.mix_high
  18.4 1.1 fusion.pick
  19.5 1.3 dynamic-slice_convert_fusion
  20.8 0.1 add.67
  20.9 0.1 add.68
  21.0 0.1 add.70
  21.0 0.9 fusion.2.order
  21.9 173.5 %shard_map.82 = bf16[2,64,4096]{2,1,0:T(8,128)(2,1)} custom-call(bf16[2,64,4096]{2,1,0:T(8,128)(2,1)} %tokens.1, bf16[2,768,256]{2,1,0:T(8,128)(2,1)} %fusion.pick, f32[2,256,1]{2,1,0:T(8,128)} %bitcast.32, f32[1,1024]{1,0:T(1,128)} %bitcast.36, bf16[2,256,768]{2,1,0:T(8,128)(2,1)} %fusion.1.mix_high, bf16[2,256,768]{2,1,0:T(8,128)(2,1)} %subtract_convert_fusion.mix_low, ...), custom_call_target="tpu_custom_call" | custom-call | flops 14495514624 | bytes 20971520 | tf_op jit(solution)/shard_map/pallas_call | solution.py:370
  195.4 2.3 %copy.49 = bf16[2,64,4096]{2,1,0:T(8,128)(2,1)} copy(bf16[2,64,4096]{2,1,0:T(8,128)(2,1)} %shard_map.82) | data formatting | bytes 2097152
  (20 shorter events, 0.2 us)
Async XLA Ops:
  1.5 9.8 %copy-start.1 = (s32[2,1,8]{2,1,0:T(1,128)S(1)}, s32[2,1,8]{2,1,0:T(1,128)}, u32[]{:S(2)}) copy-start(s32[2,1,8]{2,1,0:T(1,128)} %param.10) | copy-start | bytes 196
  10.5 1.9 copy-start

commit v4 on v3

--- a/solution.py
+++ b/solution.py
@@ -23,9 +23,7 @@
     pick,
     factor,
     gain,
-    mix_high,
-    mix_low,
-    order,
+    table,
     gate_hbm,
     up_hbm,
     down_hbm,
@@ -35,6 +33,9 @@
     rows_in,
     outgoing,
     returned,
+    mix_high,
+    mix_low,
+    order,
     recv,
     parts,
     pair_in,
@@ -220,6 +221,19 @@
         lax.fori_loop(0, feat // TILE, tile, 0)
         own_in(m).start()
 
+    def weigh(m):
+        group_rows = table.shape[1]
+        routes = (table.shape[2] - 1) // 2
+        number = lax.broadcasted_iota(jnp.int32, (group_rows, slots), 1).astype(jnp.float32)
+        spread = jnp.zeros((group_rows, slots), jnp.float32)
+        for r in range(routes):
+            spread += jnp.where(table[m, :, r : r + 1] == number, table[m, :, routes + r : routes + r + 1], 0.0)
+        top = spread.astype(jnp.bfloat16)
+        mix_high[m] = top
+        mix_low[m] = (spread - top.astype(jnp.float32)).astype(jnp.bfloat16)
+        source = lax.broadcasted_iota(jnp.int32, (group_rows, group_rows), 1).astype(jnp.float32)
+        order[m] = jnp.where(table[m, :, 2 * routes :] == source, 1.0, 0.0).astype(jnp.bfloat16)
+
     def combine(m):
         own_back(m).wait()
         for s in range(1, ep_count):
@@ -248,6 +262,8 @@
         dispatch(0, s).start()
     for m in range(1, batches):
         prepare(m)
+    for m in range(batches):
+        weigh(m)
 
     def project(m, u):
         for s in range(u * per_unit, (u + 1) * per_unit):
@@ -358,7 +374,7 @@
             ).wait_recv()
 
 
-def run_experts(tokens, pick, factor, gain, mixers, gate, up, down, ep_count):
+def run_experts(tokens, pick, factor, gain, table, gate, up, down, ep_count):
     batches, slots, group_rows = pick.shape
     feat = down.shape[1]
     units = gate.shape[1]
@@ -371,7 +387,7 @@
         functools.partial(experts_kernel, ep_count, batches),
         out_shape=jax.ShapeDtypeStruct(tokens.shape, bf16),
         in_specs=[pl.BlockSpec(memory_space=pl.ANY)]
-        + [pl.BlockSpec(memory_space=pltpu.VMEM)] * 6
+        + [pl.BlockSpec(memory_space=pltpu.VMEM)] * 4
         + [pl.BlockSpec(memory_space=pl.ANY)] * 3,
         out_specs=pl.BlockSpec(memory_space=pl.ANY),
         scratch_shapes=[
@@ -380,6 +396,9 @@
             pltpu.VMEM((batches, group_rows, feat), bf16),
             pltpu.VMEM((batches, slots, feat), bf16),
             pltpu.VMEM((batches, slots, feat), bf16),
+            pltpu.VMEM((batches, group_rows, slots), bf16),
+            pltpu.VMEM((batches, group_rows, slots), bf16),
+            pltpu.VMEM((batches, group_rows, group_rows), bf16),
             pltpu.VMEM((batches, slots, feat), bf16),
             pltpu.VMEM((batches, slots, 2 * units), bf16),
             pltpu.VMEM((count, half, 2 * units), bf16),
@@ -412,7 +431,7 @@
         cost_estimate=pl.CostEstimate(
             flops=6 * batches * slots * feat * units, bytes_accessed=20 * 2**20, transcendentals=batches * slots * units
         ),
-    )(tokens, pick, factor, gain, *mixers, gate, up, down)
+    )(tokens, pick, factor, gain, table, gate, up, down)
 
 
 def local(hidden_in, norm_gain, span_plan, route_ids, route_gates, w_gate, w_up, w_down):
@@ -439,7 +458,6 @@
     slot_place = jnp.arange(capacity, dtype=jnp.float32)
     chosen = ids == experts
     named = jnp.sum(chosen.astype(jnp.float32), 2)
-    weight = jnp.sum(jnp.where(chosen, gates, 0.0), 2)
     numbers = jnp.arange(group_rows)
     earlier = (numbers[:, None] > numbers[None, :]).astype(jnp.bfloat16)
     place = jnp.einsum("ts,mse->mte", earlier, named.astype(jnp.bfloat16), preferred_element_type=jnp.float32)
@@ -447,22 +465,18 @@
     pick = (where.transpose(0, 2, 1)[:, :, None, :] == slot_place[None, None, :, None]).astype(jnp.bfloat16)
     pick = pick.reshape(batches, slot_count, group_rows)
     plan = span_plan[:, 0]
-    table = jnp.concatenate([where, weight], 2).reshape(batches, -1, span_rows, 2 * ep_count)
-    table = jnp.take_along_axis(table, plan[:, :, None, None], axis=1).reshape(batches, group_rows, 2 * ep_count)
-    spread = jnp.where(
-        table[:, :, :ep_count, None] == slot_place, table[:, :, ep_count:, None], 0.0
-    ).reshape(batches, group_rows, slot_count)
-    high = spread.astype(jnp.bfloat16)
-    low = (spread - high.astype(jnp.float32)).astype(jnp.bfloat16)
-    source = (plan[:, :, None] * span_rows + jnp.arange(span_rows)).reshape(batches, group_rows)
-    order = (source[:, :, None] == numbers).astype(jnp.bfloat16)
+    slot = jnp.sum(jnp.where(chosen, experts * capacity + place[:, :, None, :], 0.0), -1)
+    column = jnp.broadcast_to(numbers.astype(jnp.float32)[None, :, None], (batches, group_rows, 1))
+    table = jnp.concatenate([slot, gates[..., 0], column], 2)
+    table = table.reshape(batches, -1, span_rows, 2 * routes + 1)
+    table = jnp.take_along_axis(table, plan[:, :, None, None], axis=1).reshape(batches, group_rows, -1)
 
     return run_experts(
         hidden_in,
         pick,
         facts[:, :, :1],
         gain[None, :],
-        (high, low, order),
+        table,
         w_gate[0],
         w_up[0],
         w_down[0],

time: 198 us -> 193 us (0.975)
  local copies, waits for them, and re-layouts: 8.82 us -> 4.93 us
    broadcast_in_dim x2 -> x1, local copies, waits for them, and re-layouts: 3.14 us -> 0.01 us  [local(): jnp.broadcast_to(numbers.astype(jnp.float32)[None, :, None], (batches, gr...]
    convert_element_type x3 -> x1, other arithmetic: 3.07 us -> 0.01 us  [local(): numbers.astype(jnp.float32)[None, :, None]]
where the time goes in v4:
time: 193 us; the launch traced here: 192 us
  Pallas kernels  173 us (90%)
  blocking collectives  7.19 us (4%)
  other arithmetic  6.99 us (4%)
  local copies, waits for them, and re-layouts  4.93 us (3%)
    pallas_call x1, Pallas kernels, run_experts(): pl.pallas_call(functools.partial(experts_kernel, ep_count, batches), out_...  173 us
    all_gather x1, blocking collectives, local(): facts = lax.all_gather(facts, 'dp', axis=1, tiled=True)  7.19 us

profile of v4, /device:TPU:0, one launch (start us, length us, event | category | flops | bytes accessed | tf_op | source)
XLA Modules:
  0.0 192.4 jit_solution(14902083080785783018)
XLA Ops:
  0.0 0.7 compare_and_fusion
  0.7 0.7 fusion.7
  1.4 0.1 reshape.113
  1.5 1.5 multiply_reduce_fusion
  3.0 0.1 broadcast_in_dim.51
  3.1 0.1 broadcast_in_dim.52
  3.2 0.7 convert_element_type.26
  3.9 1.3 dynamic-slice_convert_fusion
  5.1 0.1 eq.39
  5.2 0.1 copy.32
  5.3 0.1 copy.31
  5.4 0.8 copy.33
  6.2 0.1 pad_maximum_fusion
  6.3 7.2 %all_gather.3 = f32[2,256,5]{2,1,0:T(8,128)S(1)} all-gather(f32[2,64,5]{2,1,0:T(8,128)S(1)} %pad_maximum_fusion), channel_id=1, replica_groups=mesh['grp'=2,'ep'=4,'dp'=4] {'dp'}, dimensions={1}, use_global_device_ids=true | all-gather | bytes 12800 | tf_op jit(solution)/shard_map/all_gather | solution.py:452
  13.5 0.0 copy-start
  13.5 0.2 fusion.8
  13.7 0.1 copy.36
  13.8 0.1 copy.34
  14.0 0.2 add_bitcast_fusion
  14.2 0.1 select_reduce_fusion
  14.3 0.1 reshape.111
  14.4 0.6 gather_fusion
  15.0 0.2 copy.38
  15.1 0.9 bitcast_select_fusion.table
  16.0 1.1 fusion.pick
  17.1 0.0 copy-done
  17.1 173.0 %shard_map.82 = bf16[2,64,4096]{2,1,0:T(8,128)(2,1)} custom-call(bf16[2,64,4096]{2,1,0:T(8,128)(2,1)} %tokens.1, bf16[2,768,256]{2,1,0:T(8,128)(2,1)} %fusion.pick, f32[2,256,1]{2,1,0:T(8,128)} %bitcast.29, f32[1,1024]{1,0:T(1,128)} %bitcast.31, f32[2,256,5]{2,1,0:T(8,128)} %bitcast_select_fusion.table, bf16[1024,1536]{1,0:T(8,128)(2,1)} %bitcast.34, ...), custom_call_target="tpu_custom_call" | custom-call | flops 14495514624 | bytes 20971520 | tf_op jit(solution)/shard_map/pallas_call | solution.py:386
  190.1 2.3 %copy.40 = bf16[2,64,4096]{2,1,0:T(8,128)(2,1)} copy(bf16[2,64,4096]{2,1,0:T(8,128)(2,1)} %shard_map.82) | data formatting | bytes 2097152
  (9 shorter events, 0.1 us)
Async XLA Ops:
  13.5 3.5 %copy-start = (f32[2,256,5]{2,1,0:T(8,128)}, f32[2,256,5]{2,1,0:T(8,128)S(1)}, u32[]{:S(2)}) copy-start(f32[2,256,5]{2,1,0:T(8,128)S(1)} %all_gather.3) | copy-start | bytes 30724
